TPU v7x, 128 devices: a whole 4x4x4 slice. The times are simulated.
128 devices in a mesh: dp: 4 (over x), seq: 16 (over y, z_lo, core), tensor: 2 (over z_hi).
Axes of the slice: x: 4, y: 4, z: 4 (z_hi: 2, z_lo: 2; z = z_hi * 2 + z_lo), core: 2. Of those that a mesh axis runs over, the one named last changes fastest.
Arguments:
- enc_input: bfloat16 [16384, 1408], P(('dp', 'seq')), may hold values from -6 to 6
- norm_gain: float32 [1408], replicated, may hold values from 0.1 to 1.9
- fc_in: bfloat16 [1408, 6144], P(None, 'tensor'), may hold values from -0.15625 to 0.15625
- fc_out: bfloat16 [6144, 1408], P('tensor'), may hold values from -0.125 to 0.125
- final_gain: float32 [1408], replicated, may hold values from 0.1 to 1.9
- hidden_states: bfloat16 [16384, 3072], P(('dp', 'seq')), may hold values from -16 to 16
- timestep: int32 [4], P('dp'), may hold values from 0 to 999
- patch_order: int32 [256], replicated, may hold values from 0 to 255, each once
- proj_in: bfloat16 [3072, 2048], P('seq', 'tensor'), may hold values from -0.109375 to 0.109375
- proj_out: bfloat16 [1408, 2048], P('seq', 'tensor'), may hold values from -0.1875 to 0.1875
Outputs:
- state_grad: float32 [16384, 3072], P(('dp', 'seq'))
- in_grad: float32 [3072, 2048], P(('dp', 'seq'), 'tensor')
- out_grad: float32 [1408, 2048], P(('dp', 'seq'), 'tensor')
Inputs may be any that keep to these rules, and one draw needn't show every extreme that they name: `patch_order`: each of the 256 positions appears once.
All inputs are finite; a program needn't handle non-finite values.
Results may differ from a plain program's by a relative error of at most 0.02.
Values may be sent and summed in bfloat16 or wider, within the bound.
A program may use at most 128 MiB of HBM per device.

v0:
```python
import math

import jax
import jax.numpy as jnp
from jax import lax
from jax.sharding import PartitionSpec as P

TSTEPS = 1000


def layer_norm(values, gain):
    center = jnp.mean(values, axis=-1, keepdims=True)
    square = jnp.mean(values * values, axis=-1, keepdims=True)
    return (values - center) * lax.rsqrt(square - center * center + 1e-06) * gain


def on_device(
    enc_input,
    norm_gain,
    fc_in,
    fc_out,
    final_gain,
    hidden_states,
    timestep,
    patch_order,
    proj_in,
    proj_out,
):
    inputs = enc_input.astype(jnp.float32)
    normed = layer_norm(inputs, norm_gain).astype(jnp.bfloat16)
    act = jax.nn.gelu(
        jnp.dot(normed, fc_in, preferred_element_type=jnp.float32), approximate=False
    ).astype(jnp.bfloat16)
    partial_value = jnp.dot(act, fc_out, preferred_element_type=jnp.float32)
    width_all = inputs.shape[1]
    seq_count = lax.axis_size("seq")
    patches = patch_order.shape[0]
    share = patches // seq_count
    resid = inputs + lax.psum(partial_value.astype(jnp.bfloat16), "tensor").astype(jnp.float32)
    feats = layer_norm(resid, final_gain).astype(jnp.bfloat16)
    grid = feats.reshape(-1, patches, width_all)
    picked = jnp.take(grid, patch_order, axis=1).reshape(grid.shape[0], seq_count, share, width_all)
    moved = lax.all_to_all(picked, "seq", split_axis=1, concat_axis=0, tiled=True)
    target = moved.reshape(-1, width_all)
    target = target.astype(jnp.float32)
    weight_in, weight_out = (
        lax.all_gather(proj_in, "seq", axis=0, tiled=True),
        lax.all_gather(proj_out, "seq", axis=0, tiled=True),
    )
    pre = jnp.dot(hidden_states, weight_in, preferred_element_type=jnp.float32)
    pact = jax.nn.silu(pre).astype(jnp.bfloat16)
    pred_part = jnp.einsum("tk,ek->te", pact, weight_out, preferred_element_type=jnp.float32)
    pred = lax.psum(pred_part.astype(jnp.bfloat16), "tensor").astype(jnp.float32)
    inv_pred = lax.rsqrt(jnp.sum(pred * pred, axis=1, keepdims=True) + 1e-06)
    inv_target = lax.rsqrt(jnp.sum(target * target, axis=1, keepdims=True) + 1e-06)
    cosine = jnp.sum(pred * target, axis=1, keepdims=True) * inv_pred * inv_target
    weight = (0.5 + timestep.astype(jnp.float32)[0] / TSTEPS) * width_all
    dpred = (
        -weight * (inv_target * inv_pred * target - cosine * inv_pred * inv_pred * pred)
    ).astype(jnp.bfloat16)
    dact = jnp.dot(dpred, weight_out, preferred_element_type=jnp.float32)
    sigma = jax.nn.sigmoid(pre)
    dpre = (dact * sigma * (1.0 + pre * (1.0 - sigma))).astype(jnp.bfloat16)
    back_part = jnp.einsum("tk,hk->th", dpre, weight_in, preferred_element_type=jnp.float32)
    state_grad = lax.psum(back_part.astype(jnp.bfloat16), "tensor").astype(jnp.float32)
    token_count = hidden_states.shape[0] * lax.axis_size("dp") * seq_count
    factor = 1.0 / math.sqrt(token_count)
    grad_first = (
        jnp.einsum("th,tk->hk", hidden_states, dpre, preferred_element_type=jnp.float32) * factor
    )
    grad_second = jnp.einsum("te,tk->ek", dpred, pact, preferred_element_type=jnp.float32) * factor
    in_grad, out_grad = (
        lax.psum_scatter(grad_first, ("dp", "seq"), scatter_dimension=0, tiled=True),
        lax.psum_scatter(grad_second, ("dp", "seq"), scatter_dimension=0, tiled=True),
    )
    return (state_grad, in_grad, out_grad)


def solution(mesh):
    in_specs = (
        P(("dp", "seq"), None),
        P(),
        P(None, "tensor"),
        P("tensor", None),
        P(),
        P(("dp", "seq"), None),
        P("dp"),
        P(),
        P("seq", "tensor"),
        P("seq", "tensor"),
    )
    out_specs = (P(("dp", "seq"), None), P(("dp", "seq"), "tensor"), P(("dp", "seq"), "tensor"))
    return jax.shard_map(
        on_device, mesh=mesh, in_specs=in_specs, out_specs=out_specs, check_vma=False
    )
```

profile of v0, /device:TPU:1, one launch (start us, length us, event | category | flops | bytes accessed | tf_op | source)
XLA Modules:
  0.0 571.6 jit_solution(6796547223857429749)
XLA Ops:
  7.2 0.0 copy-start
  7.2 0.0 all-gather.3.cloned.1.call-start
  7.2 0.7 all-gather.3.cloned.1.call-update
  7.9 0.0 all-gather.5.cloned.1.call-start
  8.0 0.7 all-gather.5.cloned.1.call-update
  8.7 0.0 all-reduce.8.cloned.1.call-start
  8.7 1.5 convert_reduce_fusion
  10.2 17.6 %convolution_convert_fusion.2 = bf16[256,1408]{1,0:T(8,128)(2,1)} fusion(bf16[3072,1408]{1,0:T(8,128)(2,1)} %param.13, bf16[1408,3072]{1,0:T(8,128)(2,1)} %param.12, bf16[256,1408]{1,0:T(8,128)(2,1)} %param.10, f32[1408]{0:T(1024)} %param.11, f32[256]{0:T(256)S(1)} %get-tuple-element.22, f32[256]{0:T(256)S(1)} %get-tuple-element.21), kind=kOutput, calls=%fused_computation.24 | convolution fusion | flops 4482465792 | bytes 18750976 | tf_op jit(solution)/shard_map/dot_general | solution.py:34
  27.8 28.0 %all-gather.3.cloned.1.call-done = bf16[3072,1024]{1,0:T(8,128)(2,1)} async-done(((bf16[192,1024]{1,0:T(8,128)(2,1)}), bf16[3072,1024]{1,0:T(8,128)(2,1)}) %all-gather.3.cloned.1.call-update) | async-done | bytes 6291472 | tf_op jit(solution)/shard_map/all_gather | solution.py:47
  55.8 4.6 fusion.98
  60.4 33.2 %all-gather.5.cloned.1.call-done = bf16[1408,1024]{1,0:T(8,128)(2,1)} async-done(((bf16[88,1024]{1,0:T(8,128)(2,1)}), bf16[1408,1024]{1,0:T(8,128)(2,1)}) %all-gather.5.cloned.1.call-update) | async-done | bytes 2883600 | tf_op jit(solution)/shard_map/all_gather | solution.py:48
  93.6 3.9 convolution_convert_fusion.1
  97.5 0.0 all-reduce.8.cloned.1.call-update
  97.5 0.1 broadcast_in_dim.14
  97.6 56.8 %all-reduce.8.cloned.1.call-done = (bf16[256,1408]{1,0:T(8,128)(2,1)}, bf16[256,1408]{1,0:T(8,128)(2,1)}) async-done(((bf16[256,1408]{1,0:T(8,128)(2,1)}, bf16[256,1408]{1,0:T(8,128)(2,1)}), (bf16[256,1408]{1,0:T(8,128)(2,1)}, bf16[256,1408]{1,0:T(8,128)(2,1)})) %all-reduce.8.cloned.1.call-update) | async-done | bytes 1441808 | tf_op jit(solution)/shard_map/psum | solution.py:53
  154.4 1.5 fusion.54
  155.9 1.4 multiply_convert_fusion
  157.4 2.1 gather_fusion
  159.5 2.2 broadcast_select_fusion
  161.7 5.1 all-to-all-start
  166.7 0.0 all-reduce.6.cloned.1.call-start
  167.4 11.2 %all-to-all-done = bf16[1,16,16,1408]{3,2,0,1:T(8,128)(2,1)S(1)} async-done(((bf16[1,16,16,1408]{3,2,0,1:T(8,128)(2,1)}), bf16[1,16,16,1408]{3,2,0,1:T(8,128)(2,1)S(1)}, u32[]{:S(2)}, u32[]{:S(2)}) %all-to-all-start) | async-done | bytes 720928 | tf_op jit(solution)/shard_map/all_to_all | solution.py:43
  178.7 0.2 fusion.51
  178.9 0.1 rsqrt.44
  179.0 0.4 fusion.42
  179.4 1.6 fusion.46
  181.0 3.1 fusion.53
  184.1 3.0 convolution_convert_fusion
  187.1 0.0 all-reduce.6.cloned.1.call-update
  187.1 0.0 reduce-scatter.6.cloned.1.call-start
  187.2 6.3 %multiply_bitcast_fusion = f32[3072,1024]{0,1:T(8,128)} fusion(bf16[256,1024]{1,0:T(8,128)(2,1)S(1)} %fusion.53, bf16[256,3072]{1,0:T(8,128)(2,1)S(1)} %copy-done), kind=kOutput, calls=%fused_computation.1 | convolution fusion | flops 1613758464 | bytes 14680064 | tf_op jit(solution)/shard_map/th,tk->hk/dot_general | solution.py:69
  193.5 12.8 %copy.16 = f32[3072,1024]{1,0:T(8,128)} copy(f32[3072,1024]{0,1:T(8,128)} %multiply_bitcast_fusion) | data formatting | bytes 25165824
  206.3 0.0 reduce-scatter.6.cloned.1.call-update
  206.3 1.2 copy-done.5
  207.5 3.5 convolution_multiply_fusion
  211.0 167.9 %fusion = f32[24,1024]{1,0:T(8,128)S(1)} fusion(f32[1408,1024]{1,0:T(8,128)} %convolution_multiply_fusion), kind=kCustom, calls=%all-reduce-scatter | all-reduce-scatter fusion | flops 1572865 | bytes 5865984
  378.9 1.3 collective-permute-start.5
  380.2 1.3 collective-permute-start.4
  381.5 1.3 collective-permute-start.3
  382.8 1.3 collective-permute-start.2
  384.1 1.3 collective-permute-start.1
  385.5 1.9 collective-permute-start
  387.4 0.6 dynamic-slice.4
  388.7 2.0 collective-permute-done
  390.7 0.9 concatenate
  391.6 0.7 constant_dynamic-slice_fusion
  392.3 3.5 convert_element_type.70
  395.7 169.3 %reduce-scatter.6.cloned.1.call-done = f32[48,1024]{1,0:T(8,128)} async-done(((f32[3072,1024]{1,0:T(8,128)}), f32[48,1024]{1,0:T(8,128)}) %reduce-scatter.6.cloned.1.call-update) | async-done | bytes 196624
  (35 shorter events, 0.1 us)
Async XLA Ops:
  7.2 48.6 %copy-start = (bf16[256,3072]{1,0:T(8,128)(2,1)S(1)}, bf16[256,3072]{1,0:T(8,128)(2,1)}, u32[]{:S(2)}) copy-start(bf16[256,3072]{1,0:T(8,128)(2,1)} %param.15) | copy-start | bytes 4718596
  7.2 48.6 %all-gather.3.cloned.1.call-start = ((), (), s32[]{:S(2)}) async-start(), calls=%async_computation.2 | async-start | bytes 6684672 | tf_op jit(solution)/shard_map/all_gather | solution.py:47
  7.9 85.7 %all-gather.5.cloned.1.call-start = ((), (), s32[]{:S(2)}) async-start(), calls=%async_computation.3 | async-start | bytes 3063808 | tf_op jit(solution)/shard_map/all_gather | solution.py:48
  8.7 145.7 %all-reduce.8.cloned.1.call-start = ((), (), s32[]{:S(2)}) async-start(), calls=%async_computation.6 | async-start | bytes 2883584 | tf_op jit(solution)/shard_map/psum | solution.py:53
  60.4 37.1 %copy-start.3 = (f32[256,1024]{1,0:T(8,128)}, f32[256,1024]{1,0:T(8,128)S(1)}, u32[]{:S(2)}) copy-start(f32[256,1024]{1,0:T(8,128)S(1)} %fusion.98) | copy-start | bytes 3145732
  60.4 37.1 %copy-start.7 = (s32[256]{0:T(256)S(1)}, s32[256]{0:T(256)}, u32[]{:S(2)}) copy-start(s32[256]{0:T(256)} %param.17) | copy-start | bytes 3076
  60.4 94.0 %copy-start.1 = (bf16[256,1408]{1,0:T(8,128)(2,1)S(1)}, bf16[256,1408]{1,0:T(8,128)(2,1)}, u32[]{:S(2)}) copy-start(bf16[256,1408]{1,0:T(8,128)(2,1)} %param.10) | copy-start | bytes 2162692
  60.4 95.5 %copy-start.6 = (f32[1408]{0:T(1024)S(1)}, f32[1408]{0:T(1024)}, u32[]{:S(2)}) copy-start(f32[1408]{0:T(1024)} %param.14) | copy-start | bytes 16900
  159.5 19.5 %copy-start.2 = (bf16[256,1408]{1,0:T(8,128)(2,1)S(1)}, bf16[256,1408]{1,0:T(8,128)(2,1)}, u32[]{:S(2)}) copy-start(bf16[256,1408]{1,0:T(8,128)(2,1)} %get-tuple-element.15) | copy-start | bytes 2162692
  161.7 17.0 %all-to-all-start = ((bf16[1,16,16,1408]{3,2,0,1:T(8,128)(2,1)}), bf16[1,16,16,1408]{3,2,0,1:T(8,128)(2,1)S(1)}, u32[]{:S(2)}, u32[]{:S(2)}) async-start(bf16[1,16,16,1408]{3,2,0,1:T(8,128)(2,1)} %broadcast_select_fusion), calls=%async_computation | async-start | bytes 1441792 | tf_op jit(solution)/shard_map/all_to_all | solution.py:43
  166.7 225.6 %all-reduce.6.cloned.1.call-start = ((), (), s32[]{:S(2)}) async-start(), calls=%async_computation.4 | async-start | bytes 3145728 | tf_op jit(solution)/shard_map/psum | solution.py:65
  179.0 2.0 copy-start.4
  179.3 4.8 slice-start
  181.0 3.1 slice-start.1
  187.1 377.9 %reduce-scatter.6.cloned.1.call-start = ((), (), s32[]{:S(2)}) async-start(), calls=%async_computation.5 | async-start | bytes 12779520
  206.3 1.2 copy-start.5
  211.0 176.4 %copy-start.8 = (u32[128]{0:T(128)S(1)}, u32[128]{0:T(128)}, u32[]{:S(2)}) copy-start(u32[128]{0:T(128)} %constant.105) | copy-start | bytes 1540
  378.9 6.5 %collective-permute-start.5 = (f32[6,1024]{1,0:T(8,128)S(1)}, f32[6,1024]{1,0:T(8,128)S(1)}, u32[]{:S(2)}, u32[]{:S(2)}) collective-permute-start(f32[6,1024]{1,0:T(8,128)S(1)} %slice.2), channel_id=1, source_target_pairs={{0,12},{2,14},{4,16},{6,18},{8,20},{10,22},{12,24},{14,26},{16,28}... | collective-permute-start | bytes 73736
  380.2 8.4 %collective-permute-start.4 = (f32[24,1024]{1,0:T(8,128)S(1)}, f32[24,1024]{1,0:T(8,128)S(1)}, u32[]{:S(2)}, u32[]{:S(2)}) collective-permute-start(f32[24,1024]{1,0:T(8,128)S(1)} %fusion), channel_id=1, source_target_pairs={{0,10},{2,12},{4,14},{6,16},{8,18},{10,20},{12,22},{14,24},{16,26}... | collective-permute-start | bytes 294920
  381.5 7.1 %collective-permute-start.3 = (f32[24,1024]{1,0:T(8,128)S(1)}, f32[24,1024]{1,0:T(8,128)S(1)}, u32[]{:S(2)}, u32[]{:S(2)}) collective-permute-start(f32[24,1024]{1,0:T(8,128)S(1)} %fusion), channel_id=1, source_target_pairs={{0,8},{2,10},{4,12},{6,14},{8,16},{10,18},{12,20},{14,22},{16,24},... | collective-permute-start | bytes 294920
  382.8 5.8 %collective-permute-start.2 = (f32[24,1024]{1,0:T(8,128)S(1)}, f32[24,1024]{1,0:T(8,128)S(1)}, u32[]{:S(2)}, u32[]{:S(2)}) collective-permute-start(f32[24,1024]{1,0:T(8,128)S(1)} %fusion), channel_id=1, source_target_pairs={{0,6},{2,8},{4,10},{6,12},{8,14},{10,16},{12,18},{14,20},{16,22},{... | collective-permute-start | bytes 294920
  384.1 4.5 collective-permute-start.1
  385.5 5.3 collective-permute-start
Sparse Core Ops, SparseCore 0:
  9.7 46.0 all-gather.2
  57.5 36.0 all-gather.4
  97.6 56.7 all-reduce.7
  187.3 69.8 all-reduce.5
  260.0 305.0 reduce-scatter.5
where the time goes:
time: 577 us; the launch traced here: 572 us
  waiting for transfers between devices  302 us (52%)
  blocking collectives  168 us (29%)
  matrix products  41.8 us (7%)
  local copies, waits for them, and re-layouts  18.5 us (3%)
  between operations  15.4 us (3%)
  starting transfers between devices  13.7 us (2%)
  other arithmetic  12.3 us (2%)
    unnamed x12, waiting for transfers between devices  173 us
    unnamed x1, blocking collectives  168 us
    psum x1, waiting for transfers between devices, on_device(): lax.psum(pred_part.astype(jnp.bfloat16), 'tensor').astype(jnp.float32)  56.8 us
    all_gather x1, waiting for transfers between devices, on_device(): lax.all_gather(proj_out, 'seq', axis=0, tiled=True)  33.2 us
    all_gather x1, waiting for transfers between devices, on_device(): lax.all_gather(proj_in, 'seq', axis=0, tiled=True)  28 us
    dot_general x1, matrix products, on_device(): partial_value = jnp.dot(act, fc_out, preferred_element_type=jnp.float32)  17.6 us
    unnamed x27, local copies, waits for them, and re-layouts  16.2 us
  transfers between devices with their start and end apart: 12, of which 6 were waited for; matrix products, arithmetic and copies ran while one was open for 38% of the time, Pallas kernels for 0%

commit v1 on v0

v1 whole, which is shorter than its diff:
```python
import functools
import math

import jax
import jax.numpy as jnp
from jax import lax
from jax.experimental import pallas as pl
from jax.experimental.pallas import tpu as pltpu
from jax.sharding import PartitionSpec as P

TSTEPS = 1000
MESH = pl.DeviceIdType.MESH
F32 = jnp.float32
BF16 = jnp.bfloat16
ENC = 1408
HID = 3072
CH = 512
NCH = 6
SLOTS_FC = 3


def dot(a, b):
    return jnp.dot(a, b, preferred_element_type=F32)


def dot_t(a, b):
    return lax.dot_general(a, b, (((1,), (1,)), ((), ())), preferred_element_type=F32)


def layer_norm(values, gain):
    center = jnp.mean(values, axis=-1, keepdims=True)
    square = jnp.mean(values * values, axis=-1, keepdims=True)
    return (values - center) * lax.rsqrt(square - center * center + 1e-06) * gain


def kernel(
    enc, order, ng, fg, wgt, wi, wo, hid, fcin, fcout,
    zs_out, zr_out, in_out, out_out,
    fin_b, fout_b, x_s, normed, acc, fsend, frecv, feats, target,
    win, wob, wout, hid_all, hid_t,
    pre, pact, ps, pr, predo, pzs, pzr, dp_all, dp_t, dpre,
    og, gbuf, r1, s2, r2, fin, zls, zlr, cs, cr, ss_b, sr_b, zbuf,
    fsem, lsem, asem_s, asem_r, bsem_s, bsem_r, xs, xr, ts_, tr_, gs, gr, hs, hr,
):
    x = lax.axis_index("dp")
    s = lax.axis_index("seq")
    t = lax.axis_index("tensor")
    y = s // 4
    zl = (s // 2) % 2
    c = s % 2
    q = s // 2

    def dev(x_, y_, zl_, c_, t_):
        return (x_, y_ * 4 + zl_ * 2 + c_, t_)

    sib = dev(x, y, zl, 1 - c, t)
    zpart = dev(x, y, zl, c, 1 - t)
    zlpart = dev(x, y, 1 - zl, c, t)

    def heavy(d):
        return dev((x + d * (1 - c)) % 4, (y + d * c) % 4, zl, c, t)

    def light(d):
        return dev((x + d * c) % 4, (y + d * (1 - c)) % 4, zl, c, t)

    hc = x * (1 - c) + y * c
    lc = y * (1 - c) + x * c

    def rcopy(src, dst, send, recv, to):
        return pltpu.make_async_remote_copy(
            src_ref=src, dst_ref=dst, send_sem=send, recv_sem=recv, device_id=to, device_id_type=MESH
        )

    sent = []

    def go(src, dst, send, recv, to):
        cp = rcopy(src, dst, send, recv, to)
        cp.start()
        sent.append(cp)

    def got(dst, send, recv):
        rcopy(dst, dst, send, recv, sib).wait_recv()

    def fc_copies(j):
        return (
            pltpu.make_async_copy(
                fcin.at[:, pl.ds(j * CH, CH)], fin_b.at[j % SLOTS_FC], fsem.at[0, j]
            ),
            pltpu.make_async_copy(
                fcout.at[pl.ds(j * CH, CH)], fout_b.at[j % SLOTS_FC], fsem.at[1, j]
            ),
        )

    for j in range(SLOTS_FC):
        for cp in fc_copies(j):
            cp.start()
    hid_own = pltpu.make_async_copy(hid, hid_all.at[c], lsem.at[0])
    hid_own.start()

    bar = pltpu.get_barrier_semaphore()
    for d in range(1, 16):
        pl.semaphore_signal(bar, inc=1, device_id=(x, (s + d) % 16, t), device_id_type=MESH)
    for d in range(1, 4):
        pl.semaphore_signal(bar, inc=1, device_id=((x + d) % 4, s, t), device_id_type=MESH)
    pl.semaphore_signal(bar, inc=1, device_id=zpart, device_id_type=MESH)
    pl.semaphore_wait(bar, 19)

    is_src = zl * 2 + c == x
    sa = 4 - 3 * c
    sb = 1 + 3 * c

    def blk(da, db):
        return ((lc + da + 4) % 4) * sa + ((hc + db + 4) % 4) * sb

    class Gather:
        def __init__(self, src, buf, rows, ssem, rsem, lsem_):
            self.src, self.buf, self.rows, self.ss, self.rs, self.ls = src, buf, rows, ssem, rsem, lsem_

        def half(self, h):
            return self.src.at[:, pl.ds(pl.multiple_of(h * 512, 512), 512)]

        def zero_copies(self):
            own = self.buf.at[blk(0, 0)]
            return (
                rcopy(self.half(1 - c), own, self.ss.at[0], self.rs.at[0], sib),
                rcopy(self.half(0), own, self.ss.at[1], self.rs.at[0], dev(x, y, 1 - zl, 0, t)),
                rcopy(self.half(1), own, self.ss.at[2], self.rs.at[0], dev(x, y, 1 - zl, 1, t)),
            )

        def local(self):
            return pltpu.make_async_copy(self.half(c), self.buf.at[blk(0, 0)], self.ls)

        def start0(self):
            @pl.when(is_src)
            def _():
                for cp in self.zero_copies():
                    cp.start()
                self.local().start()

        def wait0(self):
            @pl.when(is_src)
            def _():
                self.local().wait()

            @pl.when(jnp.logical_not(is_src))
            def _():
                got(self.buf.at[blk(0, 0)], self.ss.at[0], self.rs.at[0])

        def end0(self):
            @pl.when(is_src)
            def _():
                for cp in self.zero_copies():
                    cp.wait_send()

        def part(self, b, h):
            n = self.rows // 2
            return self.buf.at[b, pl.ds(h * n, n)]

        def ring(self, base, at, right, left):
            ref = self.buf.at

            def first():
                go(ref[at(0)], ref[at(0)], self.ss.at[base], self.rs.at[base], right)
                go(ref[at(0)], ref[at(0)], self.ss.at[base + 1], self.rs.at[base + 1], left)

            def from_left():
                got(ref[at(-1)], self.ss.at[base], self.rs.at[base])
                go(self.part(at(-1), 0), self.part(at(-1), 0), self.ss.at[base + 2], self.rs.at[base + 2], right)

            def from_right():
                got(ref[at(1)], self.ss.at[base + 1], self.rs.at[base + 1])
                go(self.part(at(1), 1), self.part(at(1), 1), self.ss.at[base + 3], self.rs.at[base + 3], left)

            def opposite():
                got(self.part(at(2), 0), self.ss.at[base + 2], self.rs.at[base + 2])
                got(self.part(at(2), 1), self.ss.at[base + 3], self.rs.at[base + 3])

            return first, from_left, from_right, opposite

        def stage_a(self):
            return self.ring(3, lambda d: blk(d, 0), light(1), light(3))

        def stage_b(self, i, da):
            return self.ring(7 + 4 * i, lambda d: blk(da, d), heavy(1), heavy(3))

    gi = Gather(wi, win, 192, asem_s, asem_r, lsem.at[1])
    go_ = Gather(wo, wob, 96, bsem_s, bsem_r, lsem.at[2])
    both = (gi, go_)
    for g in both:
        g.start0()
    go(hid, hid_all.at[c], hs.at[0], hr.at[0], sib)

    onehot = (lax.broadcasted_iota(jnp.int32, (256, 256), 1) == order[...]).astype(F32).astype(BF16)
    xin = dot(onehot, enc[...])
    x_s[...] = xin.reshape(2, 128, ENC)
    normed[...] = layer_norm(xin, ng[...]).astype(BF16)
    acc[...] = jnp.zeros_like(acc)

    def ffn(j):
        for cp in fc_copies(j):
            cp.wait()
        h = dot(normed[...], fin_b[j % SLOTS_FC])
        a = (0.5 * h * (1.0 + lax.erf(h * math.sqrt(0.5)))).astype(BF16)
        acc[...] += dot(a, fout_b[j % SLOTS_FC]).reshape(2, 128, ENC)
        if j + SLOTS_FC < NCH:
            for cp in fc_copies(j + SLOTS_FC):
                cp.start()

    das = (0, -1, 1, 2)
    st_a = [g.stage_a() for g in both]
    st_b = [[g.stage_b(i, das[i]) for i in range(4)] for g in both]
    for g in range(2):
        both[g].wait0()
        st_a[g][0]()
        st_b[g][0][0]()
    ffn(0)
    for g in range(2):
        st_a[g][1]()
        st_b[g][1][0]()
        st_a[g][2]()
        st_b[g][2][0]()
    ffn(1)
    for g in range(2):
        st_a[g][3]()
        st_b[g][3][0]()
    ffn(2)
    ffn(3)
    for g in range(2):
        st_b[g][0][1]()
        st_b[g][0][2]()
    ffn(4)
    ffn(5)
    fsend[...] = acc[1 - t].astype(BF16)
    go(fsend, frecv, hs.at[1], hr.at[1], zpart)
    for g in range(2):
        st_b[g][1][1]()
        st_b[g][1][2]()
    hid_own.wait()
    got(hid_all.at[1 - c], hs.at[0], hr.at[0])
    for p in range(2):
        for j in range(6):
            hid_t[j * 512:(j + 1) * 512, p * 256:(p + 1) * 256] = hid_all[p, :, j * 512:(j + 1) * 512].T
    for g in range(2):
        st_b[g][2][1]()
        st_b[g][2][2]()
    got(frecv, hs.at[1], hr.at[1])
    resid = x_s[t] + (acc[t] + frecv[...].astype(F32))
    feats[...] = layer_norm(resid, fg[...]).astype(BF16).reshape(8, 16, ENC)
    hi = s // 8
    for i in range(8):
        to = 2 * i + hi

        @pl.when(to == s)
        def _():
            pltpu.make_async_copy(feats.at[i], target.at[s % 8], ts_.at[i]).start()

        @pl.when(to != s)
        def _():
            rcopy(feats.at[i], target.at[s % 8], ts_.at[i], tr_.at[s % 8], (x, to, t)).start()

    for g in range(2):
        st_b[g][3][1]()
        st_b[g][3][2]()
    for g in range(2):
        for i in range(4):
            st_b[g][i][3]()

    wout[...] = jnp.concatenate([wob[i, 0:88].astype(F32) for i in range(16)], axis=0).astype(BF16)
    for p in range(2):
        for n in range(2):
            cols = slice(n * 256, n * 256 + 256)
            v = dot(hid_all[p], win[:, :, cols].reshape(HID, 256))
            a = (v * jax.nn.sigmoid(v)).astype(BF16)
            for h in range(2):
                pre[h, p, :, cols] = v[h * 128:h * 128 + 128]
                pact[h, p, :, cols] = a[h * 128:h * 128 + 128]
    v = dot_t(pact[1 - c].reshape(256, 512), wout[...]).astype(BF16).reshape(2, 128, ENC)
    ps[...] = v
    go(ps.at[1 - t], pr.at[1 - t], xs.at[0], xr.at[0], sib)
    go(ps.at[t], pr.at[t], xs.at[1], xr.at[1], sib)
    predo[...] = dot_t(pact[c].reshape(256, 512), wout[...]).reshape(2, 128, ENC)
    got(pr.at[1 - t], xs.at[0], xr.at[0])
    pzs[...] = (predo[1 - t] + pr[1 - t].astype(F32)).astype(BF16)
    go(pzs, pzr, xs.at[2], xr.at[2], zpart)
    for i in range(8):
        to = 2 * i + hi

        @pl.when(to == s)
        def _():
            pltpu.make_async_copy(feats.at[i], target.at[s % 8], ts_.at[i]).wait()

        @pl.when(to != s)
        def _():
            rcopy(feats.at[i], target.at[s % 8], ts_.at[i], tr_.at[s % 8], (x, to, t)).wait_send()

    for i in range(8):
        @pl.when(c * 8 + i != s)
        def _():
            got(target.at[i], ts_.at[i], tr_.at[i])

    tgt = target[...].reshape(128, ENC).astype(F32)
    inv_target = lax.rsqrt(jnp.sum(tgt * tgt, axis=1, keepdims=True) + 1e-06)
    got(pr.at[t], xs.at[1], xr.at[1])
    got(pzr, xs.at[2], xr.at[2])
    pred = predo[t] + pr[t].astype(F32) + pzr[...].astype(F32)
    inv_pred = lax.rsqrt(jnp.sum(pred * pred, axis=1, keepdims=True) + 1e-06)
    cosine = jnp.sum(pred * tgt, axis=1, keepdims=True) * inv_pred * inv_target
    weight = wgt[:, 0:1]
    dp_all[c, t] = (
        -weight * (inv_target * inv_pred * tgt - cosine * inv_pred * inv_pred * pred)
    ).astype(BF16)
    go(dp_all.at[c, t], dp_all.at[c, t], xs.at[3], xr.at[3], zpart)
    go(dp_all.at[c, t], dp_all.at[c, t], xs.at[4], xr.at[4], sib)

    def back(h, p):
        d = dp_all[h, p]
        dp_t[:, pl.ds(pl.multiple_of((h * 2 + p) * 128, 128), 128)] = d.T
        dact = dot(d, wout[...])
        v = pre[h, p]
        sigma = jax.nn.sigmoid(v)
        dpre[p, h] = (dact * sigma * (1.0 + v * (1.0 - sigma))).astype(BF16)

    back(c, t)
    got(dp_all.at[1 - c, t], xs.at[4], xr.at[4])
    back(1 - c, t)
    got(dp_all.at[c, 1 - t], xs.at[3], xr.at[3])
    go(dp_all.at[c, 1 - t], dp_all.at[c, 1 - t], xs.at[5], xr.at[5], sib)
    back(c, 1 - t)
    got(dp_all.at[1 - c, 1 - t], xs.at[5], xr.at[5])
    back(1 - c, 1 - t)

    def win_rows(j):
        return win[4 * j:4 * j + 4].reshape(768, 512)

    for j in range(4):
        ss_b[j] = dot_t(dpre[1 - c].reshape(256, 512), win_rows(j)).astype(BF16)
        go(ss_b.at[j], sr_b.at[j], gs.at[j], gr.at[j], sib)

    def state(j):
        v = dot_t(dpre[c].reshape(256, 512), win_rows(j))
        got(sr_b.at[j], gs.at[j], gr.at[j])
        zbuf[j] = (v + sr_b[j].astype(F32)).astype(BF16)
        go(zbuf.at[j], zr_out.at[j], gs.at[4 + j], gr.at[4 + j], zpart)
        pltpu.make_async_copy(zbuf.at[j], zs_out.at[j], lsem.at[3 + j]).start()

    og[pl.ds(1408, 8)] = jnp.zeros((8, 512), F32)
    for i in range(4):
        og[i * 352:(i + 1) * 352] = dot(dp_t[i * 352:(i + 1) * 352], pact[...].reshape(512, 512))

    def grad(dh, dl):
        h = (hc + dh) % 4
        l = (lc + dl) % 4
        gidx = (h * (1 - c) + l * c) * 4 + l * (1 - c) + h * c
        rows = hid_t[pl.ds(pl.multiple_of(gidx * 192, 192), 192)]
        gbuf[h, l, 0:192] = dot(rows, dpre[...].reshape(512, 512)).astype(BF16)
        gbuf[h, l, 192:288] = og[pl.ds(pl.multiple_of(gidx * 88, 8), 96)].astype(BF16)
        return h, l

    lorder = (2, 1, 3, 0)
    horder = (2, 1, 3)
    for e in range(4):
        for dh in horder:
            h, l = grad(dh, lorder[e])
            n = 8 + e * 3 + dh - 1
            go(gbuf.at[h, l], r1.at[dh - 1, lorder[e]], gs.at[n], gr.at[n], heavy(dh))
        state(e)
    for e in range(4):
        dl = lorder[e]
        h, l = grad(0, dl)
        total = gbuf[h, l].astype(F32)
        for dh in horder:
            n = 8 + e * 3 + dh - 1
            got(r1.at[dh - 1, dl], gs.at[n], gr.at[n])
            total += r1[dh - 1, dl].astype(F32)
        if dl:
            s2[dl - 1] = total.astype(BF16)
            go(s2.at[dl - 1], r2.at[dl - 1], gs.at[19 + dl], gr.at[19 + dl], light(dl))
        else:
            fin[...] = total
    for dl in (2, 1, 3):
        got(r2.at[dl - 1], gs.at[19 + dl], gr.at[19 + dl])
        fin[...] += r2[dl - 1].astype(F32)
    zls[0] = fin[pl.ds(pl.multiple_of((1 - zl) * 96, 96), 96)].astype(BF16)
    zls[1] = fin[192:288].astype(BF16)
    go(zls, zlr, gs.at[23], gr.at[23], zlpart)
    got(zlr, gs.at[23], gr.at[23])
    factor = 1.0 / 128.0
    in_sum = (fin[pl.ds(pl.multiple_of(zl * 96, 96), 96)] + zlr[0].astype(F32)) * factor
    out_sum = (fin[192:288] + zlr[1].astype(F32)) * factor
    first = c == 0
    cs[0:48] = jnp.where(first, in_sum[48:96], in_sum[0:48])
    cs[48:144] = out_sum
    go(cs, cr, gs.at[24], gr.at[24], sib)
    mine = pl.ds(pl.multiple_of(c * 512, 512), 512)
    other = pl.ds(pl.multiple_of((1 - c) * 512, 512), 512)
    in_out[:, mine] = jnp.where(first, in_sum[0:48], in_sum[48:96])
    out_out[:, mine] = out_sum
    got(cr, gs.at[24], gr.at[24])
    in_out[:, other] = cr[0:48]
    out_out[:, other] = cr[48:144]

    for j in range(4):
        got(zr_out.at[j], gs.at[4 + j], gr.at[4 + j])
        pltpu.make_async_copy(zbuf.at[j], zs_out.at[j], lsem.at[3 + j]).wait()
    for g in both:
        g.end0()
    for cp in sent:
        cp.wait_send()


def on_device(
    enc_input, norm_gain, fc_in, fc_out, final_gain, hidden_states, timestep, patch_order, proj_in, proj_out
):
    order = patch_order.reshape(8, 2, 16).transpose(1, 0, 2).reshape(256, 1)
    weight = (0.5 + timestep.astype(F32) / TSTEPS) * ENC
    weight = jnp.broadcast_to(weight.reshape(1, 1), (1, 128))
    wo = jnp.pad(proj_out, ((0, 8), (0, 0)))
    vm = pl.BlockSpec(memory_space=pltpu.VMEM)
    anyspace = pl.BlockSpec(memory_space=pl.ANY)
    V = pltpu.VMEM
    D = pltpu.SemaphoreType.DMA
    scratch = [
        V((SLOTS_FC, ENC, CH), BF16), V((SLOTS_FC, CH, ENC), BF16),
        V((2, 128, ENC), F32), V((256, ENC), BF16), V((2, 128, ENC), F32),
        V((128, ENC), BF16), V((128, ENC), BF16), V((8, 16, ENC), BF16), V((8, 16, ENC), BF16),
        V((16, 192, 512), BF16), V((16, 96, 512), BF16), V((ENC, 512), BF16),
        V((2, 256, HID), BF16), V((HID, 512), BF16),
        V((2, 2, 128, 512), F32), V((2, 2, 128, 512), BF16),
        V((2, 128, ENC), BF16), V((2, 128, ENC), BF16), V((2, 128, ENC), F32),
        V((128, ENC), BF16), V((128, ENC), BF16), V((2, 2, 128, ENC), BF16), V((ENC, 512), BF16),
        V((2, 2, 128, 512), BF16),
        V((1416, 512), F32), V((4, 4, 288, 512), BF16), V((3, 4, 288, 512), BF16),
        V((3, 288, 512), BF16), V((3, 288, 512), BF16), V((288, 512), F32),
        V((2, 96, 512), BF16), V((2, 96, 512), BF16), V((144, 512), F32), V((144, 512), F32),
        V((4, 256, 768), BF16), V((4, 256, 768), BF16), V((4, 256, 768), BF16),
        D((2, NCH)), D((7,)), D((23,)), D((23,)), D((23,)), D((23,)),
        D((6,)), D((6,)), D((8,)), D((8,)), D((25,)), D((25,)), D((2,)), D((2,)),
    ]
    zs, zr, in_grad, out_full = pl.pallas_call(
        kernel,
        out_shape=(
            jax.ShapeDtypeStruct((4, 256, 768), BF16),
            jax.ShapeDtypeStruct((4, 256, 768), BF16),
            jax.ShapeDtypeStruct((48, 1024), F32),
            jax.ShapeDtypeStruct((96, 1024), F32),
        ),
        in_specs=[vm] * 7 + [anyspace] * 3,
        out_specs=(anyspace, anyspace, vm, vm),
        scratch_shapes=scratch,
        compiler_params=pltpu.CompilerParams(
            collective_id=0, has_side_effects=True, vmem_limit_bytes=62 << 20
        ),
        name="fused",
    )(
        enc_input, order, norm_gain.reshape(1, ENC), final_gain.reshape(1, ENC), weight,
        proj_in, wo, hidden_states, fc_in, fc_out,
    )
    state_grad = zs.astype(F32) + zr.astype(F32)
    state_grad = state_grad.transpose(1, 0, 2).reshape(256, HID)
    quarter = lax.axis_index("seq") % 4
    out_grad = lax.dynamic_slice_in_dim(out_full, quarter * 22, 22, axis=0)
    return (state_grad, in_grad, out_grad)


def solution(mesh):
    in_specs = (
        P(("dp", "seq"), None),
        P(),
        P(None, "tensor"),
        P("tensor", None),
        P(),
        P(("dp", "seq"), None),
        P("dp"),
        P(),
        P("seq", "tensor"),
        P("seq", "tensor"),
    )
    out_specs = (P(("dp", "seq"), None), P(("dp", "seq"), "tensor"), P(("dp", "seq"), "tensor"))
    return jax.shard_map(
        on_device, mesh=mesh, in_specs=in_specs, out_specs=out_specs, check_vma=False
    )
```

time: 577 us -> 139 us (0.24)
  waiting for transfers between devices: 302 us -> 0 us
  blocking collectives: 168 us -> 0 us
  Pallas kernels: 0 us -> 121 us
  matrix products: 41.8 us -> 0 us
  between operations: 15.4 us -> 1.34 us
  starting transfers between devices: 13.7 us -> 0 us
  other arithmetic: 12.3 us -> 2.22 us
    unnamed x12 -> x0, waiting for transfers between devices: 173 us -> none
    unnamed x1 -> x0, blocking collectives: 168 us -> none
    pallas_call x0 -> x1, Pallas kernels: none -> 121 us  [on_device(): pl.pallas_call(kernel, out_shape=(jax.ShapeDtypeStruct((4, 256, 768), BF1...]
    all_gather x2 -> x0, waiting for transfers between devices: 61.2 us -> none  [the longest x1 33.2 us: on_device(): lax.all_gather(proj_out, 'seq', axis=0, tiled=True)]
    psum x2 -> x0, waiting for transfers between devices: 56.8 us -> none  [the longest x1 56.8 us: on_device(): lax.psum(pred_part.astype(jnp.bfloat16), 'tensor').astype(jnp.float32)]
    dot_general x7 -> x0, matrix products: 41.8 us -> none  [the longest x1 17.6 us: on_device(): partial_value = jnp.dot(act, fc_out, preferred_element_type=jnp.float32)]
    unnamed x27 -> x4, local copies, waits for them, and re-layouts: 16.2 us -> 4.26 us
    all_to_all x1 -> x0, waiting for transfers between devices: 11.2 us -> none  [on_device(): lax.all_to_all(picked, 'seq', split_axis=1, concat_axis=0, tiled=True)]
  transfers between devices with their start and end apart: 12 -> 0, of which waited for: 6 -> 0; matrix products, arithmetic and copies ran while one was open for 38% -> 0% of each run, Pallas kernels for 0% -> 0%
where the time goes in v1:
time: 139 us
  Pallas kernels  121 us (87%)
  local copies, waits for them, and re-layouts  14.4 us (10%)
  other arithmetic  2.22 us (2%)
    pallas_call x1, Pallas kernels, on_device(): pl.pallas_call(kernel, out_shape=(jax.ShapeDtypeStruct((4, 256, 768), BF1...  121 us
    unnamed x4, local copies, waits for them, and re-layouts  4.26 us

profile of v1, /device:TPU:1, one launch (start us, length us, event | category | flops | bytes accessed | tf_op | source)
XLA Modules:
  0.0 138.7 jit_solution(2751160313019992104)
XLA Ops:
  0.6 1.6 %pad.4.wo = bf16[96,1024]{1,0:T(8,128)(2,1)} pad(bf16[88,1024]{1,0:T(8,128)(2,1)} %param.19, bf16[]{:T(256)} %constant.25.clone.1), padding=0_8x0_0 | pad | bytes 376834 | tf_op jit(solution)/shard_map/jit(_pad)/pad | solution.py:417
  2.3 0.8 reshape.25
  3.0 0.8 reshape.30.order
  3.8 1.3 reshape.27.ng
  5.1 1.3 reshape.28.fg
  7.0 0.5 broadcast_in_dim.8.wgt
  7.5 120.7 %fused.1 = (bf16[4,256,768]{2,1,0:T(8,128)(2,1)}, bf16[4,256,768]{2,1,0:T(8,128)(2,1)}, f32[48,1024]{1,0:T(8,128)}, f32[96,1024]{1,0:T(8,128)}) custom-call(bf16[256,1408]{1,0:T(8,128)(2,1)} %enc.1, s32[256,1]{1,0:T(8,128)} %reshape.30.order, f32[1,1408]{1,0:T(1,128)} %reshape.27.ng, f32[1,1408]{1,0:T(1,128)} %reshape.28.fg, f32[1,128]{1,0:T(1,128)} %broadcast_in_dim.8.wgt, ...), custom_call_target="tpu_custom_call" | custom-call | tf_op jit(solution)/shard_map/fused/pallas_call | solution.py:439
  128.3 1.6 %constant_dynamic-slice_fusion = f32[22,1024]{1,0:T(8,128)} fusion(f32[96,1024]{1,0:T(8,128)} %get-tuple-element.10, s32[]{:T(128)S(6)} %select_n.11), kind=kLoop, calls=%fused_computation.1 | loop fusion | bytes 180228 | tf_op jit(solution)/shard_map/dynamic_slice | solution.py:461
  129.9 2.2 %add_bitcast_fusion = f32[256,4,768]{2,0,1:T(8,128)S(1)} fusion(bf16[4,256,768]{2,1,0:T(8,128)(2,1)} %get-tuple-element.8, bf16[4,256,768]{2,1,0:T(8,128)(2,1)} %get-tuple-element.7), kind=kLoop, calls=%fused_computation | loop fusion | flops 2359296 | bytes 6291456 | tf_op jit(solution)/shard_map/transpose | solution.py:459
  132.1 2.4 %copy.15 = f32[256,4,768]{0,2,1:T(8,128)} copy(f32[256,4,768]{2,0,1:T(8,128)S(1)} %add_bitcast_fusion) | data formatting | bytes 6291456 | tf_op jit(solution)/shard_map/transpose | solution.py:459
  134.5 0.0 copy-start
  134.5 3.6 %copy.16 = f32[256,3072]{1,0:T(8,128)} copy(f32[256,3072]{0,1:T(8,128)} %bitcast.5) | data formatting | bytes 6291456
  138.0 0.0 copy-done
  138.0 0.7 copy.19
  (1 shorter events, 0.0 us)
Async XLA Ops:
  134.5 3.6 %copy-start = (f32[48,1024]{1,0:T(8,128)S(1)}, f32[48,1024]{1,0:T(8,128)}, u32[]{:S(2)}) copy-start(f32[48,1024]{1,0:T(8,128)} %get-tuple-element.18) | copy-start | bytes 589828

commit v2 on v1

--- a/solution.py
+++ b/solution.py
@@ -34,9 +34,9 @@
 
 
 def kernel(
-    enc, order, ng, fg, wgt, wi, wo, hid, fcin, fcout,
+    enc, order, ng, fg, steps, wi, wo_raw, hid, fcin, fcout,
     zs_out, zr_out, in_out, out_out,
-    fin_b, fout_b, x_s, normed, acc, fsend, frecv, feats, target,
+    wo, fin_b, fout_b, x_s, normed, acc, fsend, frecv, feats, target,
     win, wob, wout, hid_all, hid_t,
     pre, pact, ps, pr, predo, pzs, pzr, dp_all, dp_t, dpre,
     og, gbuf, r1, s2, r2, fin, zls, zlr, cs, cr, ss_b, sr_b, zbuf,
@@ -97,6 +97,9 @@
     hid_own = pltpu.make_async_copy(hid, hid_all.at[c], lsem.at[0])
     hid_own.start()
 
+    wo[0:88] = wo_raw[...]
+    wo[88:96] = jnp.zeros((8, 1024), BF16)
+
     bar = pltpu.get_barrier_semaphore()
     for d in range(1, 16):
         pl.semaphore_signal(bar, inc=1, device_id=(x, (s + d) % 16, t), device_id_type=MESH)
@@ -190,10 +193,11 @@
         g.start0()
     go(hid, hid_all.at[c], hs.at[0], hr.at[0], sib)
 
-    onehot = (lax.broadcasted_iota(jnp.int32, (256, 256), 1) == order[...]).astype(F32).astype(BF16)
-    xin = dot(onehot, enc[...])
+    onehot = (lax.broadcasted_iota(jnp.int32, (256, 256), 0) == order[...].reshape(1, 256)).astype(F32)
+    xin = dot(onehot.T.astype(BF16), enc[...])
+    xin = jnp.swapaxes(xin.reshape(8, 2, 16, ENC), 0, 1).reshape(256, ENC)
     x_s[...] = xin.reshape(2, 128, ENC)
-    normed[...] = layer_norm(xin, ng[...]).astype(BF16)
+    normed[...] = layer_norm(xin, ng[...].reshape(1, ENC)).astype(BF16)
     acc[...] = jnp.zeros_like(acc)
 
     def ffn(j):
@@ -245,7 +249,7 @@
         st_b[g][2][2]()
     got(frecv, hs.at[1], hr.at[1])
     resid = x_s[t] + (acc[t] + frecv[...].astype(F32))
-    feats[...] = layer_norm(resid, fg[...]).astype(BF16).reshape(8, 16, ENC)
+    feats[...] = layer_norm(resid, fg[...].reshape(1, ENC)).astype(BF16).reshape(8, 16, ENC)
     hi = s // 8
     for i in range(8):
         to = 2 * i + hi
@@ -305,7 +309,7 @@
     pred = predo[t] + pr[t].astype(F32) + pzr[...].astype(F32)
     inv_pred = lax.rsqrt(jnp.sum(pred * pred, axis=1, keepdims=True) + 1e-06)
     cosine = jnp.sum(pred * tgt, axis=1, keepdims=True) * inv_pred * inv_target
-    weight = wgt[:, 0:1]
+    weight = (0.5 + steps[0].astype(F32) / TSTEPS) * ENC
     dp_all[c, t] = (
         -weight * (inv_target * inv_pred * tgt - cosine * inv_pred * inv_pred * pred)
     ).astype(BF16)
@@ -340,8 +344,8 @@
         v = dot_t(dpre[c].reshape(256, 512), win_rows(j))
         got(sr_b.at[j], gs.at[j], gr.at[j])
         zbuf[j] = (v + sr_b[j].astype(F32)).astype(BF16)
-        go(zbuf.at[j], zr_out.at[j], gs.at[4 + j], gr.at[4 + j], zpart)
-        pltpu.make_async_copy(zbuf.at[j], zs_out.at[j], lsem.at[3 + j]).start()
+        go(zbuf.at[j], zr_out.at[:, pl.ds(j * 768, 768)], gs.at[4 + j], gr.at[4 + j], zpart)
+        pltpu.make_async_copy(zbuf.at[j], zs_out.at[:, pl.ds(j * 768, 768)], lsem.at[3 + j]).start()
 
     og[pl.ds(1408, 8)] = jnp.zeros((8, 512), F32)
     for i in range(4):
@@ -388,20 +392,27 @@
     in_sum = (fin[pl.ds(pl.multiple_of(zl * 96, 96), 96)] + zlr[0].astype(F32)) * factor
     out_sum = (fin[192:288] + zlr[1].astype(F32)) * factor
     first = c == 0
+
+    def quarter(i):
+        lo = jnp.where(i % 2 == 0, out_sum[0:22], out_sum[22:44])
+        hi_ = jnp.where(i % 2 == 0, out_sum[44:66], out_sum[66:88])
+        return jnp.where(i < 2, lo, hi_)
+
     cs[0:48] = jnp.where(first, in_sum[48:96], in_sum[0:48])
-    cs[48:144] = out_sum
+    cs[48:70] = quarter(zl * 2 + 1 - c)
+    cs[70:72] = jnp.zeros((2, 512), F32)
     go(cs, cr, gs.at[24], gr.at[24], sib)
     mine = pl.ds(pl.multiple_of(c * 512, 512), 512)
     other = pl.ds(pl.multiple_of((1 - c) * 512, 512), 512)
     in_out[:, mine] = jnp.where(first, in_sum[0:48], in_sum[48:96])
-    out_out[:, mine] = out_sum
+    out_out[:, mine] = quarter(zl * 2 + c)
     got(cr, gs.at[24], gr.at[24])
     in_out[:, other] = cr[0:48]
-    out_out[:, other] = cr[48:144]
+    out_out[:, other] = cr[48:70]
 
     for j in range(4):
-        got(zr_out.at[j], gs.at[4 + j], gr.at[4 + j])
-        pltpu.make_async_copy(zbuf.at[j], zs_out.at[j], lsem.at[3 + j]).wait()
+        got(zr_out.at[:, pl.ds(j * 768, 768)], gs.at[4 + j], gr.at[4 + j])
+        pltpu.make_async_copy(zbuf.at[j], zs_out.at[:, pl.ds(j * 768, 768)], lsem.at[3 + j]).wait()
     for g in both:
         g.end0()
     for cp in sent:
@@ -411,16 +422,12 @@
 def on_device(
     enc_input, norm_gain, fc_in, fc_out, final_gain, hidden_states, timestep, patch_order, proj_in, proj_out
 ):
-    order = patch_order.reshape(8, 2, 16).transpose(1, 0, 2).reshape(256, 1)
-    weight = (0.5 + timestep.astype(F32) / TSTEPS) * ENC
-    weight = jnp.broadcast_to(weight.reshape(1, 1), (1, 128))
-    wo = jnp.pad(proj_out, ((0, 8), (0, 0)))
     vm = pl.BlockSpec(memory_space=pltpu.VMEM)
     anyspace = pl.BlockSpec(memory_space=pl.ANY)
     V = pltpu.VMEM
     D = pltpu.SemaphoreType.DMA
     scratch = [
-        V((SLOTS_FC, ENC, CH), BF16), V((SLOTS_FC, CH, ENC), BF16),
+        V((96, 1024), BF16), V((SLOTS_FC, ENC, CH), BF16), V((SLOTS_FC, CH, ENC), BF16),
         V((2, 128, ENC), F32), V((256, ENC), BF16), V((2, 128, ENC), F32),
         V((128, ENC), BF16), V((128, ENC), BF16), V((8, 16, ENC), BF16), V((8, 16, ENC), BF16),
         V((16, 192, 512), BF16), V((16, 96, 512), BF16), V((ENC, 512), BF16),
@@ -431,20 +438,20 @@
         V((2, 2, 128, 512), BF16),
         V((1416, 512), F32), V((4, 4, 288, 512), BF16), V((3, 4, 288, 512), BF16),
         V((3, 288, 512), BF16), V((3, 288, 512), BF16), V((288, 512), F32),
-        V((2, 96, 512), BF16), V((2, 96, 512), BF16), V((144, 512), F32), V((144, 512), F32),
+        V((2, 96, 512), BF16), V((2, 96, 512), BF16), V((72, 512), F32), V((72, 512), F32),
         V((4, 256, 768), BF16), V((4, 256, 768), BF16), V((4, 256, 768), BF16),
         D((2, NCH)), D((7,)), D((23,)), D((23,)), D((23,)), D((23,)),
         D((6,)), D((6,)), D((8,)), D((8,)), D((25,)), D((25,)), D((2,)), D((2,)),
     ]
-    zs, zr, in_grad, out_full = pl.pallas_call(
+    zs, zr, in_grad, out_grad = pl.pallas_call(
         kernel,
         out_shape=(
-            jax.ShapeDtypeStruct((4, 256, 768), BF16),
-            jax.ShapeDtypeStruct((4, 256, 768), BF16),
+            jax.ShapeDtypeStruct((256, HID), BF16),
+            jax.ShapeDtypeStruct((256, HID), BF16),
             jax.ShapeDtypeStruct((48, 1024), F32),
-            jax.ShapeDtypeStruct((96, 1024), F32),
+            jax.ShapeDtypeStruct((22, 1024), F32),
         ),
-        in_specs=[vm] * 7 + [anyspace] * 3,
+        in_specs=[vm] * 4 + [pl.BlockSpec(memory_space=pltpu.SMEM)] + [vm] * 2 + [anyspace] * 3,
         out_specs=(anyspace, anyspace, vm, vm),
         scratch_shapes=scratch,
         compiler_params=pltpu.CompilerParams(
@@ -452,13 +459,10 @@
         ),
         name="fused",
     )(
-        enc_input, order, norm_gain.reshape(1, ENC), final_gain.reshape(1, ENC), weight,
-        proj_in, wo, hidden_states, fc_in, fc_out,
+        enc_input, patch_order, norm_gain, final_gain, timestep,
+        proj_in, proj_out, hidden_states, fc_in, fc_out,
     )
     state_grad = zs.astype(F32) + zr.astype(F32)
-    state_grad = state_grad.transpose(1, 0, 2).reshape(256, HID)
-    quarter = lax.axis_index("seq") % 4
-    out_grad = lax.dynamic_slice_in_dim(out_full, quarter * 22, 22, axis=0)
     return (state_grad, in_grad, out_grad)
 
 

time: 139 us -> 127 us (0.914)
  local copies, waits for them, and re-layouts: 14.4 us -> 1.33 us
  other arithmetic: 2.22 us -> 4.11 us
    add x0 -> x1, other arithmetic: none -> 4.11 us  [on_device(): state_grad = zs.astype(F32) + zr.astype(F32)]
    reshape x4 -> x0, local copies, waits for them, and re-layouts: 4.1 us -> none  [the longest x2 1.52 us: on_device(): order = patch_order.reshape(8, 2, 16).transpose(1, 0, 2).reshape(256, 1)]
    unnamed x4 -> x6, local copies, waits for them, and re-layouts: 4.26 us -> 1.33 us
    transpose x2 -> x0, local copies, waits for them, and re-layouts: 2.36 us -> none  [the longest x1 2.36 us: on_device(): state_grad = state_grad.transpose(1, 0, 2).reshape(256, HID)]
    transpose x1 -> x0, other arithmetic: 2.22 us -> none  [on_device(): state_grad = state_grad.transpose(1, 0, 2).reshape(256, HID)]
    pad x1 -> x0, local copies, waits for them, and re-layouts: 1.61 us -> none  [on_device(): wo = jnp.pad(proj_out, ((0, 8), (0, 0)))]
    dynamic_slice x1 -> x0, local copies, waits for them, and re-layouts: 1.57 us -> none  [on_device(): out_grad = lax.dynamic_slice_in_dim(out_full, quarter * 22, 22, axis=0)]
where the time goes in v2:
time: 127 us
  Pallas kernels  120 us (94%)
  other arithmetic  4.11 us (3%)
  local copies, waits for them, and re-layouts  1.33 us (1%)
  between operations  1.31 us (1%)
    pallas_call x1, Pallas kernels, on_device(): pl.pallas_call(kernel, out_shape=(jax.ShapeDtypeStruct((256, HID), BF16),...  120 us
    add x1, other arithmetic, on_device(): state_grad = zs.astype(F32) + zr.astype(F32)  4.11 us

profile of v2, /device:TPU:1, one launch (start us, length us, event | category | flops | bytes accessed | tf_op | source)
XLA Modules:
  0.0 127.2 jit_solution(14808515902909166816)
XLA Ops:
  1.3 120.5 %fused.1 = (bf16[256,3072]{1,0:T(8,128)(2,1)}, bf16[256,3072]{1,0:T(8,128)(2,1)}, f32[48,1024]{1,0:T(8,128)}, f32[22,1024]{1,0:T(8,128)}) custom-call(bf16[256,1408]{1,0:T(8,128)(2,1)} %enc.1, s32[256]{0:T(256)} %order.1, f32[1408]{0:T(1024)} %ng.1, f32[1408]{0:T(1024)} %fg.1, s32[1]{0:T(128)S(6)} %copy.15.steps, bf16[192,1024]{1,0:T(8,128)(2,1)} %wi.1, ...), custom_call_target="tpu_custom_call" | custom-call | tf_op jit(solution)/shard_map/fused/pallas_call | solution.py:446
  121.7 0.0 copy-start
  121.8 0.0 copy-start.1
  121.8 4.1 %convert_add_fusion = f32[256,3072]{1,0:T(8,128)} fusion(bf16[256,3072]{1,0:T(8,128)(2,1)} %get-tuple-element.8, bf16[256,3072]{1,0:T(8,128)(2,1)} %get-tuple-element.7), kind=kLoop, calls=%fused_computation | loop fusion | flops 2359296 | bytes 6291456 | tf_op jit(solution)/shard_map/add | solution.py:465
  125.9 0.0 copy-done
  125.9 0.7 copy.16
  126.6 0.0 copy-done.1
  126.6 0.6 copy.17
Async XLA Ops:
  121.7 4.1 %copy-start = (f32[48,1024]{1,0:T(8,128)S(1)}, f32[48,1024]{1,0:T(8,128)}, u32[]{:S(2)}) copy-start(f32[48,1024]{1,0:T(8,128)} %get-tuple-element.15) | copy-start | bytes 589828
  121.8 4.8 %copy-start.1 = (f32[22,1024]{1,0:T(8,128)S(1)}, f32[22,1024]{1,0:T(8,128)}, u32[]{:S(2)}) copy-start(f32[22,1024]{1,0:T(8,128)} %get-tuple-element.16) | copy-start | bytes 270340

commit v3 on v2

--- a/solution.py
+++ b/solution.py
@@ -39,7 +39,7 @@
     wo, fin_b, fout_b, x_s, normed, acc, fsend, frecv, feats, target,
     win, wob, wout, hid_all, hid_t,
     pre, pact, ps, pr, predo, pzs, pzr, dp_all, dp_t, dpre,
-    og, gbuf, r1, s2, r2, fin, zls, zlr, cs, cr, ss_b, sr_b, zbuf,
+    og, gbuf, rh, r1, s2, r2, fin, cs, cr, ss_b, sr_b, zbuf,
     fsem, lsem, asem_s, asem_r, bsem_s, bsem_r, xs, xr, ts_, tr_, gs, gr, hs, hr,
 ):
     x = lax.axis_index("dp")
@@ -108,30 +108,33 @@
     pl.semaphore_signal(bar, inc=1, device_id=zpart, device_id_type=MESH)
     pl.semaphore_wait(bar, 19)
 
-    is_src = zl * 2 + c == x
-    sa = 4 - 3 * c
-    sb = 1 + 3 * c
-
-    def blk(da, db):
-        return ((lc + da + 4) % 4) * sa + ((hc + db + 4) % 4) * sb
+    is_src = c == x // 2
 
     class Gather:
         def __init__(self, src, buf, rows, ssem, rsem, lsem_):
             self.src, self.buf, self.rows, self.ss, self.rs, self.ls = src, buf, rows, ssem, rsem, lsem_
 
+        def piece(self, da, db, z):
+            yy = (y + da * (1 - c) + db * c + 4) % 4
+            xx = (x + da * c + db * (1 - c) + 4) % 4
+            if z == 2:
+                return self.buf.at[yy, :, xx]
+            return self.buf.at[yy, zl if z == 0 else 1 - zl, xx]
+
         def half(self, h):
-            return self.src.at[:, pl.ds(pl.multiple_of(h * 512, 512), 512)]
+            n = self.rows
+            return self.src.at[pl.ds(pl.multiple_of((x % 2) * n, n), n), pl.ds(pl.multiple_of(h * 512, 512), 512)]
 
         def zero_copies(self):
-            own = self.buf.at[blk(0, 0)]
+            own = self.piece(0, 0, 0)
             return (
                 rcopy(self.half(1 - c), own, self.ss.at[0], self.rs.at[0], sib),
-                rcopy(self.half(0), own, self.ss.at[1], self.rs.at[0], dev(x, y, 1 - zl, 0, t)),
-                rcopy(self.half(1), own, self.ss.at[2], self.rs.at[0], dev(x, y, 1 - zl, 1, t)),
+                rcopy(self.half(0), own, self.ss.at[1], self.rs.at[1], dev(x, y, 1 - zl, 0, t)),
+                rcopy(self.half(1), own, self.ss.at[2], self.rs.at[1], dev(x, y, 1 - zl, 1, t)),
             )
 
         def local(self):
-            return pltpu.make_async_copy(self.half(c), self.buf.at[blk(0, 0)], self.ls)
+            return pltpu.make_async_copy(self.half(c), self.piece(0, 0, 0), self.ls)
 
         def start0(self):
             @pl.when(is_src)
@@ -140,54 +143,79 @@
                     cp.start()
                 self.local().start()
 
-        def wait0(self):
-            @pl.when(is_src)
-            def _():
-                self.local().wait()
-
-            @pl.when(jnp.logical_not(is_src))
-            def _():
-                got(self.buf.at[blk(0, 0)], self.ss.at[0], self.rs.at[0])
-
         def end0(self):
             @pl.when(is_src)
             def _():
                 for cp in self.zero_copies():
                     cp.wait_send()
 
-        def part(self, b, h):
-            n = self.rows // 2
-            return self.buf.at[b, pl.ds(h * n, n)]
-
-        def ring(self, base, at, right, left):
-            ref = self.buf.at
-
-            def first():
-                go(ref[at(0)], ref[at(0)], self.ss.at[base], self.rs.at[base], right)
-                go(ref[at(0)], ref[at(0)], self.ss.at[base + 1], self.rs.at[base + 1], left)
-
-            def from_left():
-                got(ref[at(-1)], self.ss.at[base], self.rs.at[base])
-                go(self.part(at(-1), 0), self.part(at(-1), 0), self.ss.at[base + 2], self.rs.at[base + 2], right)
-
-            def from_right():
-                got(ref[at(1)], self.ss.at[base + 1], self.rs.at[base + 1])
-                go(self.part(at(1), 1), self.part(at(1), 1), self.ss.at[base + 3], self.rs.at[base + 3], left)
-
-            def opposite():
-                got(self.part(at(2), 0), self.ss.at[base + 2], self.rs.at[base + 2])
-                got(self.part(at(2), 1), self.ss.at[base + 3], self.rs.at[base + 3])
-
-            return first, from_left, from_right, opposite
-
-        def stage_a(self):
-            return self.ring(3, lambda d: blk(d, 0), light(1), light(3))
-
-        def stage_b(self, i, da):
-            return self.ring(7 + 4 * i, lambda d: blk(da, d), heavy(1), heavy(3))
-
-    gi = Gather(wi, win, 192, asem_s, asem_r, lsem.at[1])
-    go_ = Gather(wo, wob, 96, bsem_s, bsem_r, lsem.at[2])
+        def put(self, n, ref, to):
+            go(ref, ref, self.ss.at[n], self.rs.at[n], to)
+
+        def take(self, n, ref):
+            got(ref, self.ss.at[n], self.rs.at[n])
+
+        def native(self):
+            @pl.when(is_src)
+            def _():
+                self.local().wait()
+
+            @pl.when(jnp.logical_not(is_src))
+            def _():
+                self.take(0, self.piece(0, 0, 0))
+
+            self.begin(0)
+
+        def foreign(self):
+            self.take(1, self.piece(0, 0, 1))
+            self.begin(1)
+
+        def begin(self, z):
+            own = self.piece(0, 0, z)
+            self.put(3 + 4 * z, own, light(1))
+            self.put(4 + 4 * z, own, light(3))
+            self.put(5 + 4 * z, own, heavy(1))
+            self.put(6 + 4 * z, own, heavy(3))
+
+        def light_near(self):
+            self.take(3, self.piece(-1, 0, 0))
+            self.put(11, self.piece(-1, 0, 0), light(1))
+            self.take(8, self.piece(1, 0, 1))
+            self.put(12, self.piece(1, 0, 1), light(3))
+            self.take(7, self.piece(-1, 0, 1))
+            self.take(4, self.piece(1, 0, 0))
+            for k, da in ((13, -1), (15, 1)):
+                self.put(k, self.piece(da, 0, 2), heavy(1))
+                self.put(k + 1, self.piece(da, 0, 2), heavy(3))
+
+        def light_far(self):
+            self.take(11, self.piece(2, 0, 0))
+            self.take(12, self.piece(2, 0, 1))
+            self.put(17, self.piece(2, 0, 2), heavy(1))
+            self.put(18, self.piece(2, 0, 2), heavy(3))
+
+        def heavy_own(self):
+            self.take(5, self.piece(0, -1, 0))
+            self.put(19, self.piece(0, -1, 0), heavy(1))
+            self.take(10, self.piece(0, 1, 1))
+            self.put(20, self.piece(0, 1, 1), heavy(3))
+
+        def heavy_other(self, i):
+            da = (-1, 1, 2)[i]
+            self.take(13 + 2 * i, self.piece(da, -1, 2))
+            self.put(21 + 2 * i, self.piece(da, -1, 0), heavy(1))
+            self.take(14 + 2 * i, self.piece(da, 1, 2))
+            self.put(22 + 2 * i, self.piece(da, 1, 1), heavy(3))
+
+        def finish(self):
+            self.take(9, self.piece(0, -1, 1))
+            self.take(6, self.piece(0, 1, 0))
+            for k, da in ((19, 0), (21, -1), (23, 1), (25, 2)):
+                self.take(k, self.piece(da, 2, 0))
+                self.take(k + 1, self.piece(da, 2, 1))
+
+    gi = Gather(wi, win, 96, asem_s, asem_r, lsem.at[1])
+    go_ = Gather(wo, wob, 48, bsem_s, bsem_r, lsem.at[2])
     both = (gi, go_)
     for g in both:
         g.start0()
@@ -210,43 +238,55 @@
             for cp in fc_copies(j + SLOTS_FC):
                 cp.start()
 
-    das = (0, -1, 1, 2)
-    st_a = [g.stage_a() for g in both]
-    st_b = [[g.stage_b(i, das[i]) for i in range(4)] for g in both]
-    for g in range(2):
-        both[g].wait0()
-        st_a[g][0]()
-        st_b[g][0][0]()
+    for g in both:
+        g.native()
+    for g in both:
+        g.foreign()
     ffn(0)
-    for g in range(2):
-        st_a[g][1]()
-        st_b[g][1][0]()
-        st_a[g][2]()
-        st_b[g][2][0]()
+    gi.light_near()
     ffn(1)
-    for g in range(2):
-        st_a[g][3]()
-        st_b[g][3][0]()
+    gi.light_far()
+    go_.light_near()
     ffn(2)
+    gi.heavy_own()
+    go_.light_far()
     ffn(3)
-    for g in range(2):
-        st_b[g][0][1]()
-        st_b[g][0][2]()
+    gi.heavy_other(0)
     ffn(4)
+    gi.heavy_other(1)
     ffn(5)
     fsend[...] = acc[1 - t].astype(BF16)
     go(fsend, frecv, hs.at[1], hr.at[1], zpart)
-    for g in range(2):
-        st_b[g][1][1]()
-        st_b[g][1][2]()
+    gi.heavy_other(2)
+    go_.heavy_own()
     hid_own.wait()
     got(hid_all.at[1 - c], hs.at[0], hr.at[0])
     for p in range(2):
         for j in range(6):
             hid_t[j * 512:(j + 1) * 512, p * 256:(p + 1) * 256] = hid_all[p, :, j * 512:(j + 1) * 512].T
-    for g in range(2):
-        st_b[g][2][1]()
-        st_b[g][2][2]()
+    go_.heavy_other(0)
+    go_.heavy_other(1)
+    gi.finish()
+    go_.heavy_other(2)
+
+    for p in range(2):
+        for n in range(2):
+            cols = slice(n * 256, n * 256 + 256)
+            v = dot(hid_all[p], win[:, :, :, :, cols].reshape(HID, 256))
+            a = (v * jax.nn.sigmoid(v)).astype(BF16)
+            for h in range(2):
+                pre[h, p, :, cols] = v[h * 128:h * 128 + 128]
+                pact[h, p, :, cols] = a[h * 128:h * 128 + 128]
+    go_.finish()
+    wout[...] = jnp.concatenate(
+        [wob[i, z, 2 * k:2 * k + 2].reshape(96, 512)[0:88].astype(F32) for i in range(4) for z in range(2) for k in range(2)],
+        axis=0,
+    ).astype(BF16)
+    v = dot_t(pact[1 - c].reshape(256, 512), wout[...]).astype(BF16).reshape(2, 128, ENC)
+    ps[...] = v
+    go(ps.at[1 - t], pr.at[1 - t], xs.at[0], xr.at[0], sib)
+    go(ps.at[t], pr.at[t], xs.at[1], xr.at[1], sib)
+    predo[...] = dot_t(pact[c].reshape(256, 512), wout[...]).reshape(2, 128, ENC)
     got(frecv, hs.at[1], hr.at[1])
     resid = x_s[t] + (acc[t] + frecv[...].astype(F32))
     feats[...] = layer_norm(resid, fg[...].reshape(1, ENC)).astype(BF16).reshape(8, 16, ENC)
@@ -262,27 +302,6 @@
         def _():
             rcopy(feats.at[i], target.at[s % 8], ts_.at[i], tr_.at[s % 8], (x, to, t)).start()
 
-    for g in range(2):
-        st_b[g][3][1]()
-        st_b[g][3][2]()
-    for g in range(2):
-        for i in range(4):
-            st_b[g][i][3]()
-
-    wout[...] = jnp.concatenate([wob[i, 0:88].astype(F32) for i in range(16)], axis=0).astype(BF16)
-    for p in range(2):
-        for n in range(2):
-            cols = slice(n * 256, n * 256 + 256)
-            v = dot(hid_all[p], win[:, :, cols].reshape(HID, 256))
-            a = (v * jax.nn.sigmoid(v)).astype(BF16)
-            for h in range(2):
-                pre[h, p, :, cols] = v[h * 128:h * 128 + 128]
-                pact[h, p, :, cols] = a[h * 128:h * 128 + 128]
-    v = dot_t(pact[1 - c].reshape(256, 512), wout[...]).astype(BF16).reshape(2, 128, ENC)
-    ps[...] = v
-    go(ps.at[1 - t], pr.at[1 - t], xs.at[0], xr.at[0], sib)
-    go(ps.at[t], pr.at[t], xs.at[1], xr.at[1], sib)
-    predo[...] = dot_t(pact[c].reshape(256, 512), wout[...]).reshape(2, 128, ENC)
     got(pr.at[1 - t], xs.at[0], xr.at[0])
     pzs[...] = (predo[1 - t] + pr[1 - t].astype(F32)).astype(BF16)
     go(pzs, pzr, xs.at[2], xr.at[2], zpart)
@@ -334,7 +353,7 @@
     back(1 - c, 1 - t)
 
     def win_rows(j):
-        return win[4 * j:4 * j + 4].reshape(768, 512)
+        return win[j].reshape(768, 512)
 
     for j in range(4):
         ss_b[j] = dot_t(dpre[1 - c].reshape(256, 512), win_rows(j)).astype(BF16)
@@ -361,54 +380,60 @@
         return h, l
 
     lorder = (2, 1, 3, 0)
-    horder = (2, 1, 3)
     for e in range(4):
-        for dh in horder:
-            h, l = grad(dh, lorder[e])
-            n = 8 + e * 3 + dh - 1
-            go(gbuf.at[h, l], r1.at[dh - 1, lorder[e]], gs.at[n], gr.at[n], heavy(dh))
+        dl = lorder[e]
+        h, l = grad(2, dl)
+        go(gbuf.at[h, l, pl.ds(0, 144)], rh.at[0, dl], gs.at[8 + 4 * e], gr.at[8 + 4 * e], heavy(1))
+        go(gbuf.at[h, l, pl.ds(144, 144)], rh.at[1, dl], gs.at[9 + 4 * e], gr.at[9 + 4 * e], heavy(3))
+    for e in range(4):
+        dl = lorder[e]
         state(e)
+        for k, dh in ((0, 1), (1, 3)):
+            h, l = grad(dh, dl)
+            part = pl.ds(k * 144, 144)
+            n = 8 + 4 * e + k
+            got(rh.at[k, dl], gs.at[n], gr.at[n])
+            gbuf[h, l, part] = (gbuf[h, l, part].astype(F32) + rh[k, dl].astype(F32)).astype(BF16)
+            go(gbuf.at[h, l], r1.at[k, dl], gs.at[n + 2], gr.at[n + 2], heavy(dh))
     for e in range(4):
         dl = lorder[e]
         h, l = grad(0, dl)
         total = gbuf[h, l].astype(F32)
-        for dh in horder:
-            n = 8 + e * 3 + dh - 1
-            got(r1.at[dh - 1, dl], gs.at[n], gr.at[n])
-            total += r1[dh - 1, dl].astype(F32)
+        for k in range(2):
+            n = 10 + 4 * e + k
+            got(r1.at[k, dl], gs.at[n], gr.at[n])
+            total += r1[k, dl].astype(F32)
         if dl:
             s2[dl - 1] = total.astype(BF16)
-            go(s2.at[dl - 1], r2.at[dl - 1], gs.at[19 + dl], gr.at[19 + dl], light(dl))
+            go(s2.at[dl - 1], r2.at[dl - 1], gs.at[23 + dl], gr.at[23 + dl], light(dl))
         else:
             fin[...] = total
     for dl in (2, 1, 3):
-        got(r2.at[dl - 1], gs.at[19 + dl], gr.at[19 + dl])
+        got(r2.at[dl - 1], gs.at[23 + dl], gr.at[23 + dl])
         fin[...] += r2[dl - 1].astype(F32)
-    zls[0] = fin[pl.ds(pl.multiple_of((1 - zl) * 96, 96), 96)].astype(BF16)
-    zls[1] = fin[192:288].astype(BF16)
-    go(zls, zlr, gs.at[23], gr.at[23], zlpart)
-    got(zlr, gs.at[23], gr.at[23])
+
+    def rows_for(zl_, c_):
+        even = c_ == 0
+        lo = jnp.where(even, fin[192:214], fin[214:236])
+        hi_ = jnp.where(even, fin[236:258], fin[258:280])
+        return fin[pl.ds(pl.multiple_of(zl_ * 96 + c_ * 48, 48), 48)], jnp.where(zl_ == 0, lo, hi_)
+
+    dests = ((1 - zl, 1 - c), (1 - zl, c), (zl, 1 - c))
+    for k in range(3):
+        a, b = rows_for(*dests[k])
+        cs[k, 0:48] = a.astype(BF16)
+        cs[k, 48:80] = jnp.concatenate([b, jnp.zeros((10, 512), F32)], axis=0).astype(BF16)
+        go(cs.at[k], cr.at[k], gs.at[27 + k], gr.at[27 + k], dev(x, y, dests[k][0], dests[k][1], t))
     factor = 1.0 / 128.0
-    in_sum = (fin[pl.ds(pl.multiple_of(zl * 96, 96), 96)] + zlr[0].astype(F32)) * factor
-    out_sum = (fin[192:288] + zlr[1].astype(F32)) * factor
-    first = c == 0
-
-    def quarter(i):
-        lo = jnp.where(i % 2 == 0, out_sum[0:22], out_sum[22:44])
-        hi_ = jnp.where(i % 2 == 0, out_sum[44:66], out_sum[66:88])
-        return jnp.where(i < 2, lo, hi_)
-
-    cs[0:48] = jnp.where(first, in_sum[48:96], in_sum[0:48])
-    cs[48:70] = quarter(zl * 2 + 1 - c)
-    cs[70:72] = jnp.zeros((2, 512), F32)
-    go(cs, cr, gs.at[24], gr.at[24], sib)
     mine = pl.ds(pl.multiple_of(c * 512, 512), 512)
     other = pl.ds(pl.multiple_of((1 - c) * 512, 512), 512)
-    in_out[:, mine] = jnp.where(first, in_sum[0:48], in_sum[48:96])
-    out_out[:, mine] = quarter(zl * 2 + c)
-    got(cr, gs.at[24], gr.at[24])
-    in_out[:, other] = cr[0:48]
-    out_out[:, other] = cr[48:70]
+    a, b = rows_for(zl, c)
+    for k in range(3):
+        got(cr.at[k], gs.at[27 + k], gr.at[27 + k])
+    in_out[:, mine] = (a + cr[1, 0:48].astype(F32)) * factor
+    out_out[:, mine] = (b + cr[1, 48:80].astype(F32)[0:22]) * factor
+    in_out[:, other] = (cr[0, 0:48].astype(F32) + cr[2, 0:48].astype(F32)) * factor
+    out_out[:, other] = (cr[0, 48:80].astype(F32) + cr[2, 48:80].astype(F32))[0:22] * factor
 
     for j in range(4):
         got(zr_out.at[:, pl.ds(j * 768, 768)], gs.at[4 + j], gr.at[4 + j])
@@ -430,18 +455,18 @@
         V((96, 1024), BF16), V((SLOTS_FC, ENC, CH), BF16), V((SLOTS_FC, CH, ENC), BF16),
         V((2, 128, ENC), F32), V((256, ENC), BF16), V((2, 128, ENC), F32),
         V((128, ENC), BF16), V((128, ENC), BF16), V((8, 16, ENC), BF16), V((8, 16, ENC), BF16),
-        V((16, 192, 512), BF16), V((16, 96, 512), BF16), V((ENC, 512), BF16),
+        V((4, 2, 4, 96, 512), BF16), V((4, 2, 4, 48, 512), BF16), V((ENC, 512), BF16),
         V((2, 256, HID), BF16), V((HID, 512), BF16),
         V((2, 2, 128, 512), F32), V((2, 2, 128, 512), BF16),
         V((2, 128, ENC), BF16), V((2, 128, ENC), BF16), V((2, 128, ENC), F32),
         V((128, ENC), BF16), V((128, ENC), BF16), V((2, 2, 128, ENC), BF16), V((ENC, 512), BF16),
         V((2, 2, 128, 512), BF16),
-        V((1416, 512), F32), V((4, 4, 288, 512), BF16), V((3, 4, 288, 512), BF16),
+        V((1416, 512), F32), V((4, 4, 288, 512), BF16), V((2, 4, 144, 512), BF16), V((2, 4, 288, 512), BF16),
         V((3, 288, 512), BF16), V((3, 288, 512), BF16), V((288, 512), F32),
-        V((2, 96, 512), BF16), V((2, 96, 512), BF16), V((72, 512), F32), V((72, 512), F32),
+        V((3, 80, 512), BF16), V((3, 80, 512), BF16),
         V((4, 256, 768), BF16), V((4, 256, 768), BF16), V((4, 256, 768), BF16),
-        D((2, NCH)), D((7,)), D((23,)), D((23,)), D((23,)), D((23,)),
-        D((6,)), D((6,)), D((8,)), D((8,)), D((25,)), D((25,)), D((2,)), D((2,)),
+        D((2, NCH)), D((7,)), D((27,)), D((27,)), D((27,)), D((27,)),
+        D((6,)), D((6,)), D((8,)), D((8,)), D((30,)), D((30,)), D((2,)), D((2,)),
     ]
     zs, zr, in_grad, out_grad = pl.pallas_call(
         kernel,

time: 127 us -> 117 us (0.921)
  Pallas kernels: 120 us -> 111 us
    pallas_call x1, Pallas kernels: 120 us -> 111 us  [on_device(): pl.pallas_call(kernel, out_shape=(jax.ShapeDtypeStruct((256, HID), BF16),...]
where the time goes in v3:
time: 117 us
  Pallas kernels  111 us (95%)
  other arithmetic  4.11 us (4%)
  local copies, waits for them, and re-layouts  1.33 us (1%)
  between operations  1.31 us (1%)
    pallas_call x1, Pallas kernels, on_device(): pl.pallas_call(kernel, out_shape=(jax.ShapeDtypeStruct((256, HID), BF16),...  111 us
    add x1, other arithmetic, on_device(): state_grad = zs.astype(F32) + zr.astype(F32)  4.11 us

profile of v3, /device:TPU:1, one launch (start us, length us, event | category | flops | bytes accessed | tf_op | source)
XLA Modules:
  0.0 117.3 jit_solution(12465863092314015810)
XLA Ops:
  1.3 110.6 %fused.1 = (bf16[256,3072]{1,0:T(8,128)(2,1)}, bf16[256,3072]{1,0:T(8,128)(2,1)}, f32[48,1024]{1,0:T(8,128)}, f32[22,1024]{1,0:T(8,128)}) custom-call(bf16[256,1408]{1,0:T(8,128)(2,1)} %enc.1, s32[256]{0:T(256)} %order.1, f32[1408]{0:T(1024)} %ng.1, f32[1408]{0:T(1024)} %fg.1, s32[1]{0:T(128)S(6)} %copy.15.steps, bf16[192,1024]{1,0:T(8,128)(2,1)} %wi.1, ...), custom_call_target="tpu_custom_call" | custom-call | tf_op jit(solution)/shard_map/fused/pallas_call | solution.py:471
  111.9 0.0 copy-start
  111.9 0.0 copy-start.1
  111.9 4.1 %convert_add_fusion = f32[256,3072]{1,0:T(8,128)} fusion(bf16[256,3072]{1,0:T(8,128)(2,1)} %get-tuple-element.8, bf16[256,3072]{1,0:T(8,128)(2,1)} %get-tuple-element.7), kind=kLoop, calls=%fused_computation | loop fusion | flops 2359296 | bytes 6291456 | tf_op jit(solution)/shard_map/add | solution.py:490
  116.0 0.0 copy-done
  116.0 0.7 copy.16
  116.7 0.0 copy-done.1
  116.7 0.6 copy.17
Async XLA Ops:
  111.9 4.1 %copy-start = (f32[48,1024]{1,0:T(8,128)S(1)}, f32[48,1024]{1,0:T(8,128)}, u32[]{:S(2)}) copy-start(f32[48,1024]{1,0:T(8,128)} %get-tuple-element.15) | copy-start | bytes 589828
  111.9 4.8 %copy-start.1 = (f32[22,1024]{1,0:T(8,128)S(1)}, f32[22,1024]{1,0:T(8,128)}, u32[]{:S(2)}) copy-start(f32[22,1024]{1,0:T(8,128)} %get-tuple-element.16) | copy-start | bytes 270340

commit v4 on v3

--- a/solution.py
+++ b/solution.py
@@ -106,6 +106,14 @@
     for d in range(1, 4):
         pl.semaphore_signal(bar, inc=1, device_id=((x + d) % 4, s, t), device_id_type=MESH)
     pl.semaphore_signal(bar, inc=1, device_id=zpart, device_id_type=MESH)
+
+    onehot = (lax.broadcasted_iota(jnp.int32, (256, 256), 0) == order[...].reshape(1, 256)).astype(F32)
+    xin = dot(onehot.T.astype(BF16), enc[...])
+    xin = jnp.swapaxes(xin.reshape(8, 2, 16, ENC), 0, 1).reshape(256, ENC)
+    x_s[...] = xin.reshape(2, 128, ENC)
+    normed[...] = layer_norm(xin, ng[...].reshape(1, ENC)).astype(BF16)
+    acc[...] = jnp.zeros_like(acc)
+
     pl.semaphore_wait(bar, 19)
 
     is_src = c == x // 2
@@ -174,14 +182,13 @@
             own = self.piece(0, 0, z)
             self.put(3 + 4 * z, own, light(1))
             self.put(4 + 4 * z, own, light(3))
+            self.put(11 + z, own, light(2))
             self.put(5 + 4 * z, own, heavy(1))
             self.put(6 + 4 * z, own, heavy(3))
 
         def light_near(self):
             self.take(3, self.piece(-1, 0, 0))
-            self.put(11, self.piece(-1, 0, 0), light(1))
             self.take(8, self.piece(1, 0, 1))
-            self.put(12, self.piece(1, 0, 1), light(3))
             self.take(7, self.piece(-1, 0, 1))
             self.take(4, self.piece(1, 0, 0))
             for k, da in ((13, -1), (15, 1)):
@@ -193,6 +200,7 @@
             self.take(12, self.piece(2, 0, 1))
             self.put(17, self.piece(2, 0, 2), heavy(1))
             self.put(18, self.piece(2, 0, 2), heavy(3))
+            self.put(25, self.piece(2, 0, 2), heavy(2))
 
         def heavy_own(self):
             self.take(5, self.piece(0, -1, 0))
@@ -201,7 +209,7 @@
             self.put(20, self.piece(0, 1, 1), heavy(3))
 
         def heavy_other(self, i):
-            da = (-1, 1, 2)[i]
+            da = (-1, 1)[i]
             self.take(13 + 2 * i, self.piece(da, -1, 2))
             self.put(21 + 2 * i, self.piece(da, -1, 0), heavy(1))
             self.take(14 + 2 * i, self.piece(da, 1, 2))
@@ -210,9 +218,11 @@
         def finish(self):
             self.take(9, self.piece(0, -1, 1))
             self.take(6, self.piece(0, 1, 0))
-            for k, da in ((19, 0), (21, -1), (23, 1), (25, 2)):
+            for k, da in ((19, 0), (21, -1), (23, 1)):
                 self.take(k, self.piece(da, 2, 0))
                 self.take(k + 1, self.piece(da, 2, 1))
+            for k, db in ((17, -1), (18, 1), (25, 2)):
+                self.take(k, self.piece(2, db, 2))
 
     gi = Gather(wi, win, 96, asem_s, asem_r, lsem.at[1])
     go_ = Gather(wo, wob, 48, bsem_s, bsem_r, lsem.at[2])
@@ -220,13 +230,6 @@
     for g in both:
         g.start0()
     go(hid, hid_all.at[c], hs.at[0], hr.at[0], sib)
-
-    onehot = (lax.broadcasted_iota(jnp.int32, (256, 256), 0) == order[...].reshape(1, 256)).astype(F32)
-    xin = dot(onehot.T.astype(BF16), enc[...])
-    xin = jnp.swapaxes(xin.reshape(8, 2, 16, ENC), 0, 1).reshape(256, ENC)
-    x_s[...] = xin.reshape(2, 128, ENC)
-    normed[...] = layer_norm(xin, ng[...].reshape(1, ENC)).astype(BF16)
-    acc[...] = jnp.zeros_like(acc)
 
     def ffn(j):
         for cp in fc_copies(j):
@@ -257,7 +260,6 @@
     ffn(5)
     fsend[...] = acc[1 - t].astype(BF16)
     go(fsend, frecv, hs.at[1], hr.at[1], zpart)
-    gi.heavy_other(2)
     go_.heavy_own()
     hid_own.wait()
     got(hid_all.at[1 - c], hs.at[0], hr.at[0])
@@ -267,7 +269,6 @@
     go_.heavy_other(0)
     go_.heavy_other(1)
     gi.finish()
-    go_.heavy_other(2)
 
     for p in range(2):
         for n in range(2):
@@ -343,28 +344,61 @@
         sigma = jax.nn.sigmoid(v)
         dpre[p, h] = (dact * sigma * (1.0 + v * (1.0 - sigma))).astype(BF16)
 
+    def win_rows(j):
+        return win[j].reshape(768, 512)
+
+    def to_sib(j):
+        return rcopy(ss_b.at[j], sr_b.at[j], gs.at[j], gr.at[j], sib)
+
+    def to_pair(j):
+        return rcopy(zbuf.at[j], zr_out.at[:, pl.ds(j * 768, 768)], gs.at[4 + j], gr.at[4 + j], zpart)
+
+    def keep(j):
+        return pltpu.make_async_copy(zbuf.at[j], zs_out.at[:, pl.ds(j * 768, 768)], lsem.at[3 + j])
+
+    def theirs():
+        for j in range(4):
+            ss_b[j] = dot_t(dpre[1 - c].reshape(256, 512), win_rows(j)).astype(BF16)
+            to_sib(j).start()
+
+    def ours():
+        for j in range(4):
+            v = dot_t(dpre[c].reshape(256, 512), win_rows(j))
+            got(sr_b.at[j], gs.at[j], gr.at[j])
+            zbuf[j] = (v + sr_b[j].astype(F32)).astype(BF16)
+
+    def send_ours():
+        for j in range(4):
+            to_pair(j).start()
+            keep(j).start()
+
+    early = c == t
     back(c, t)
     got(dp_all.at[1 - c, t], xs.at[4], xr.at[4])
     back(1 - c, t)
+
+    @pl.when(jnp.logical_not(early))
+    def _():
+        theirs()
+
+    @pl.when(early)
+    def _():
+        ours()
+
     got(dp_all.at[c, 1 - t], xs.at[3], xr.at[3])
     go(dp_all.at[c, 1 - t], dp_all.at[c, 1 - t], xs.at[5], xr.at[5], sib)
+
+    @pl.when(early)
+    def _():
+        send_ours()
+
     back(c, 1 - t)
     got(dp_all.at[1 - c, 1 - t], xs.at[5], xr.at[5])
     back(1 - c, 1 - t)
 
-    def win_rows(j):
-        return win[j].reshape(768, 512)
-
-    for j in range(4):
-        ss_b[j] = dot_t(dpre[1 - c].reshape(256, 512), win_rows(j)).astype(BF16)
-        go(ss_b.at[j], sr_b.at[j], gs.at[j], gr.at[j], sib)
-
-    def state(j):
-        v = dot_t(dpre[c].reshape(256, 512), win_rows(j))
-        got(sr_b.at[j], gs.at[j], gr.at[j])
-        zbuf[j] = (v + sr_b[j].astype(F32)).astype(BF16)
-        go(zbuf.at[j], zr_out.at[:, pl.ds(j * 768, 768)], gs.at[4 + j], gr.at[4 + j], zpart)
-        pltpu.make_async_copy(zbuf.at[j], zs_out.at[:, pl.ds(j * 768, 768)], lsem.at[3 + j]).start()
+    @pl.when(early)
+    def _():
+        theirs()
 
     og[pl.ds(1408, 8)] = jnp.zeros((8, 512), F32)
     for i in range(4):
@@ -385,9 +419,14 @@
         h, l = grad(2, dl)
         go(gbuf.at[h, l, pl.ds(0, 144)], rh.at[0, dl], gs.at[8 + 4 * e], gr.at[8 + 4 * e], heavy(1))
         go(gbuf.at[h, l, pl.ds(144, 144)], rh.at[1, dl], gs.at[9 + 4 * e], gr.at[9 + 4 * e], heavy(3))
+
+    @pl.when(jnp.logical_not(early))
+    def _():
+        ours()
+        send_ours()
+
     for e in range(4):
         dl = lorder[e]
-        state(e)
         for k, dh in ((0, 1), (1, 3)):
             h, l = grad(dh, dl)
             part = pl.ds(k * 144, 144)
@@ -436,12 +475,40 @@
     out_out[:, other] = (cr[0, 48:80].astype(F32) + cr[2, 48:80].astype(F32))[0:22] * factor
 
     for j in range(4):
-        got(zr_out.at[:, pl.ds(j * 768, 768)], gs.at[4 + j], gr.at[4 + j])
-        pltpu.make_async_copy(zbuf.at[j], zs_out.at[:, pl.ds(j * 768, 768)], lsem.at[3 + j]).wait()
+        to_pair(j).wait_recv()
+        to_pair(j).wait_send()
+        to_sib(j).wait_send()
+        keep(j).wait()
     for g in both:
         g.end0()
     for cp in sent:
         cp.wait_send()
+
+
+def close_kernel(a, b, in_ref, out_ref, state, in_grad, out_grad):
+    state[...] = a[...].astype(F32) + b[...].astype(F32)
+
+    @pl.when(pl.program_id(0) == 0)
+    def _():
+        in_grad[...] = in_ref[...]
+        out_grad[...] = out_ref[...]
+
+
+def close(a, b, in_grad, out_grad):
+    rows = pl.BlockSpec((64, HID), lambda i: (i, 0))
+    whole = [pl.BlockSpec(v.shape, lambda i: (0, 0)) for v in (in_grad, out_grad)]
+    return pl.pallas_call(
+        close_kernel,
+        grid=(4,),
+        out_shape=(
+            jax.ShapeDtypeStruct((256, HID), F32),
+            jax.ShapeDtypeStruct(in_grad.shape, F32),
+            jax.ShapeDtypeStruct(out_grad.shape, F32),
+        ),
+        in_specs=[rows, rows] + whole,
+        out_specs=(rows, *whole),
+        name="close",
+    )(a, b, in_grad, out_grad)
 
 
 def on_device(
@@ -465,7 +532,7 @@
         V((3, 288, 512), BF16), V((3, 288, 512), BF16), V((288, 512), F32),
         V((3, 80, 512), BF16), V((3, 80, 512), BF16),
         V((4, 256, 768), BF16), V((4, 256, 768), BF16), V((4, 256, 768), BF16),
-        D((2, NCH)), D((7,)), D((27,)), D((27,)), D((27,)), D((27,)),
+        D((2, NCH)), D((7,)), D((26,)), D((26,)), D((26,)), D((26,)),
         D((6,)), D((6,)), D((8,)), D((8,)), D((30,)), D((30,)), D((2,)), D((2,)),
     ]
     zs, zr, in_grad, out_grad = pl.pallas_call(
@@ -487,8 +554,7 @@
         enc_input, patch_order, norm_gain, final_gain, timestep,
         proj_in, proj_out, hidden_states, fc_in, fc_out,
     )
-    state_grad = zs.astype(F32) + zr.astype(F32)
-    return (state_grad, in_grad, out_grad)
+    return close(zs, zr, in_grad, out_grad)
 
 
 def solution(mesh):

time: 117 us -> 113 us (0.966)
  other arithmetic: 4.11 us -> 0 us
  local copies, waits for them, and re-layouts: 1.33 us -> 0 us
    pallas_call x0 -> x1, Pallas kernels: none -> 4.4 us  [close(): pl.pallas_call(close_kernel, grid=(4,), out_shape=(jax.ShapeDtypeStruct((...]
    add x1 -> x0, other arithmetic: 4.11 us -> none  [on_device(): state_grad = zs.astype(F32) + zr.astype(F32)]
    pallas_call x1, Pallas kernels: 111 us -> 107 us  [on_device(): pl.pallas_call(kernel, out_shape=(jax.ShapeDtypeStruct((256, HID), BF16),...]
    unnamed x6 -> x0, local copies, waits for them, and re-layouts: 1.33 us -> none
where the time goes in v4:
time: 113 us
  Pallas kernels  112 us (99%)
  between operations  1.29 us (1%)
    pallas_call x1, Pallas kernels, on_device(): pl.pallas_call(kernel, out_shape=(jax.ShapeDtypeStruct((256, HID), BF16),...  107 us
    pallas_call x1, Pallas kernels, close(): pl.pallas_call(close_kernel, grid=(4,), out_shape=(jax.ShapeDtypeStruct((...  4.4 us

profile of v4, /device:TPU:1, one launch (start us, length us, event | category | flops | bytes accessed | tf_op | source)
XLA Modules:
  0.0 113.1 jit_solution(3082442827065622182)
XLA Ops:
  1.3 107.5 %fused.1 = (bf16[256,3072]{1,0:T(8,128)(2,1)}, bf16[256,3072]{1,0:T(8,128)(2,1)}, f32[48,1024]{1,0:T(8,128)}, f32[22,1024]{1,0:T(8,128)}) custom-call(bf16[256,1408]{1,0:T(8,128)(2,1)} %enc.1, s32[256]{0:T(256)} %order.1, f32[1408]{0:T(1024)} %ng.1, f32[1408]{0:T(1024)} %fg.1, s32[1]{0:T(128)S(6)} %copy.13.steps, bf16[192,1024]{1,0:T(8,128)(2,1)} %wi.1, ...), custom_call_target="tpu_custom_call" | custom-call | tf_op jit(solution)/shard_map/fused/pallas_call | solution.py:538
  108.7 4.4 %close.1 = (f32[256,3072]{1,0:T(8,128)}, f32[48,1024]{1,0:T(8,128)}, f32[22,1024]{1,0:T(8,128)}) custom-call(bf16[256,3072]{1,0:T(8,128)(2,1)} %get-tuple-element.7.a, bf16[256,3072]{1,0:T(8,128)(2,1)} %get-tuple-element.8.b, f32[48,1024]{1,0:T(8,128)} %get-tuple-element.9.in_ref, f32[22,1024]{1,0:T(8,128)} %get-tuple-element.10.out_ref), custom_call_target="tpu_custom_call" | custom-call | tf_op jit(solution)/shard_map/close/pallas_call | solution.py:500

commit v5 on v4

--- a/solution.py
+++ b/solution.py
@@ -263,11 +263,23 @@
     go_.heavy_own()
     hid_own.wait()
     got(hid_all.at[1 - c], hs.at[0], hr.at[0])
-    for p in range(2):
-        for j in range(6):
-            hid_t[j * 512:(j + 1) * 512, p * 256:(p + 1) * 256] = hid_all[p, :, j * 512:(j + 1) * 512].T
     go_.heavy_other(0)
     go_.heavy_other(1)
+    got(frecv, hs.at[1], hr.at[1])
+    resid = x_s[t] + (acc[t] + frecv[...].astype(F32))
+    feats[...] = layer_norm(resid, fg[...].reshape(1, ENC)).astype(BF16).reshape(8, 16, ENC)
+    hi = s // 8
+    for i in range(8):
+        to = 2 * i + hi
+
+        @pl.when(to == s)
+        def _():
+            pltpu.make_async_copy(feats.at[i], target.at[s % 8], ts_.at[i]).start()
+
+        @pl.when(to != s)
+        def _():
+            rcopy(feats.at[i], target.at[s % 8], ts_.at[i], tr_.at[s % 8], (x, to, t)).start()
+
     gi.finish()
 
     for p in range(2):
@@ -283,29 +295,20 @@
         [wob[i, z, 2 * k:2 * k + 2].reshape(96, 512)[0:88].astype(F32) for i in range(4) for z in range(2) for k in range(2)],
         axis=0,
     ).astype(BF16)
-    v = dot_t(pact[1 - c].reshape(256, 512), wout[...]).astype(BF16).reshape(2, 128, ENC)
-    ps[...] = v
+    ps[1 - t] = dot_t(pact[1 - c, 1 - t], wout[...]).astype(BF16)
     go(ps.at[1 - t], pr.at[1 - t], xs.at[0], xr.at[0], sib)
+    predo[1 - t] = dot_t(pact[c, 1 - t], wout[...])
+    ps[t] = dot_t(pact[1 - c, t], wout[...]).astype(BF16)
     go(ps.at[t], pr.at[t], xs.at[1], xr.at[1], sib)
-    predo[...] = dot_t(pact[c].reshape(256, 512), wout[...]).reshape(2, 128, ENC)
-    got(frecv, hs.at[1], hr.at[1])
-    resid = x_s[t] + (acc[t] + frecv[...].astype(F32))
-    feats[...] = layer_norm(resid, fg[...].reshape(1, ENC)).astype(BF16).reshape(8, 16, ENC)
-    hi = s // 8
-    for i in range(8):
-        to = 2 * i + hi
-
-        @pl.when(to == s)
-        def _():
-            pltpu.make_async_copy(feats.at[i], target.at[s % 8], ts_.at[i]).start()
-
-        @pl.when(to != s)
-        def _():
-            rcopy(feats.at[i], target.at[s % 8], ts_.at[i], tr_.at[s % 8], (x, to, t)).start()
-
     got(pr.at[1 - t], xs.at[0], xr.at[0])
-    pzs[...] = (predo[1 - t] + pr[1 - t].astype(F32)).astype(BF16)
-    go(pzs, pzr, xs.at[2], xr.at[2], zpart)
+    halves = (slice(0, 64), slice(64, 128))
+    for r, rows in enumerate(halves):
+        pzs[rows] = (predo[1 - t, rows] + pr[1 - t, rows].astype(F32)).astype(BF16)
+        go(pzs.at[rows], pzr.at[rows], xs.at[2 + 4 * r], xr.at[2 + 4 * r], zpart)
+    predo[t] = dot_t(pact[c, t], wout[...])
+    for p in range(2):
+        for j in range(6):
+            hid_t[j * 512:(j + 1) * 512, p * 256:(p + 1) * 256] = hid_all[p, :, j * 512:(j + 1) * 512].T
     for i in range(8):
         to = 2 * i + hi
 
@@ -325,15 +328,16 @@
     tgt = target[...].reshape(128, ENC).astype(F32)
     inv_target = lax.rsqrt(jnp.sum(tgt * tgt, axis=1, keepdims=True) + 1e-06)
     got(pr.at[t], xs.at[1], xr.at[1])
-    got(pzr, xs.at[2], xr.at[2])
-    pred = predo[t] + pr[t].astype(F32) + pzr[...].astype(F32)
-    inv_pred = lax.rsqrt(jnp.sum(pred * pred, axis=1, keepdims=True) + 1e-06)
-    cosine = jnp.sum(pred * tgt, axis=1, keepdims=True) * inv_pred * inv_target
     weight = (0.5 + steps[0].astype(F32) / TSTEPS) * ENC
-    dp_all[c, t] = (
-        -weight * (inv_target * inv_pred * tgt - cosine * inv_pred * inv_pred * pred)
-    ).astype(BF16)
-    go(dp_all.at[c, t], dp_all.at[c, t], xs.at[3], xr.at[3], zpart)
+    for r, rows in enumerate(halves):
+        got(pzr.at[rows], xs.at[2 + 4 * r], xr.at[2 + 4 * r])
+        pred = predo[t, rows] + pr[t, rows].astype(F32) + pzr[rows].astype(F32)
+        ry = lax.rsqrt(jnp.sum(pred * pred, axis=1, keepdims=True) + 1e-06)
+        rz = inv_target[rows]
+        cosine = jnp.sum(pred * tgt[rows], axis=1, keepdims=True) * ry * rz
+        dp_all[c, t, rows] = (-weight * (rz * ry * tgt[rows] - cosine * ry * ry * pred)).astype(BF16)
+        part = dp_all.at[c, t, rows]
+        go(part, part, xs.at[3 + 4 * r], xr.at[3 + 4 * r], zpart)
     go(dp_all.at[c, t], dp_all.at[c, t], xs.at[4], xr.at[4], sib)
 
     def back(h, p):
@@ -385,15 +389,18 @@
     def _():
         ours()
 
-    got(dp_all.at[c, 1 - t], xs.at[3], xr.at[3])
-    go(dp_all.at[c, 1 - t], dp_all.at[c, 1 - t], xs.at[5], xr.at[5], sib)
+    for r, rows in enumerate(halves):
+        part = dp_all.at[c, 1 - t, rows]
+        got(part, xs.at[3 + 4 * r], xr.at[3 + 4 * r])
+        go(part, part, xs.at[5 + 3 * r], xr.at[5 + 3 * r], sib)
 
     @pl.when(early)
     def _():
         send_ours()
 
     back(c, 1 - t)
-    got(dp_all.at[1 - c, 1 - t], xs.at[5], xr.at[5])
+    for r, rows in enumerate(halves):
+        got(dp_all.at[1 - c, 1 - t, rows], xs.at[5 + 3 * r], xr.at[5 + 3 * r])
     back(1 - c, 1 - t)
 
     @pl.when(early)
@@ -495,11 +502,11 @@
 
 
 def close(a, b, in_grad, out_grad):
-    rows = pl.BlockSpec((64, HID), lambda i: (i, 0))
+    rows = pl.BlockSpec((128, HID), lambda i: (i, 0))
     whole = [pl.BlockSpec(v.shape, lambda i: (0, 0)) for v in (in_grad, out_grad)]
     return pl.pallas_call(
         close_kernel,
-        grid=(4,),
+        grid=(2,),
         out_shape=(
             jax.ShapeDtypeStruct((256, HID), F32),
             jax.ShapeDtypeStruct(in_grad.shape, F32),
@@ -533,7 +540,7 @@
         V((3, 80, 512), BF16), V((3, 80, 512), BF16),
         V((4, 256, 768), BF16), V((4, 256, 768), BF16), V((4, 256, 768), BF16),
         D((2, NCH)), D((7,)), D((26,)), D((26,)), D((26,)), D((26,)),
-        D((6,)), D((6,)), D((8,)), D((8,)), D((30,)), D((30,)), D((2,)), D((2,)),
+        D((9,)), D((9,)), D((8,)), D((8,)), D((30,)), D((30,)), D((2,)), D((2,)),
     ]
     zs, zr, in_grad, out_grad = pl.pallas_call(
         kernel,

time: 113 us -> 106 us (0.938)
  Pallas kernels: 112 us -> 105 us
    pallas_call x1, Pallas kernels: 107 us -> 101 us  [on_device(): pl.pallas_call(kernel, out_shape=(jax.ShapeDtypeStruct((256, HID), BF16),...]
where the time goes in v5:
time: 106 us
  Pallas kernels  105 us (99%)
  between operations  1.29 us (1%)
    pallas_call x1, Pallas kernels, on_device(): pl.pallas_call(kernel, out_shape=(jax.ShapeDtypeStruct((256, HID), BF16),...  101 us
    pallas_call x1, Pallas kernels, close(): pl.pallas_call(close_kernel, grid=(2,), out_shape=(jax.ShapeDtypeStruct((...  3.36 us

profile of v5, /device:TPU:1, one launch (start us, length us, event | category | flops | bytes accessed | tf_op | source)
XLA Modules:
  0.0 105.9 jit_solution(101588778854753775)
XLA Ops:
  1.3 101.2 %fused.1 = (bf16[256,3072]{1,0:T(8,128)(2,1)}, bf16[256,3072]{1,0:T(8,128)(2,1)}, f32[48,1024]{1,0:T(8,128)}, f32[22,1024]{1,0:T(8,128)}) custom-call(bf16[256,1408]{1,0:T(8,128)(2,1)} %enc.1, s32[256]{0:T(256)} %order.1, f32[1408]{0:T(1024)} %ng.1, f32[1408]{0:T(1024)} %fg.1, s32[1]{0:T(128)S(6)} %copy.13.steps, bf16[192,1024]{1,0:T(8,128)(2,1)} %wi.1, ...), custom_call_target="tpu_custom_call" | custom-call | tf_op jit(solution)/shard_map/fused/pallas_call | solution.py:545
  102.5 3.4 %close.1 = (f32[256,3072]{1,0:T(8,128)}, f32[48,1024]{1,0:T(8,128)}, f32[22,1024]{1,0:T(8,128)}) custom-call(bf16[256,3072]{1,0:T(8,128)(2,1)} %get-tuple-element.7.a, bf16[256,3072]{1,0:T(8,128)(2,1)} %get-tuple-element.8.b, f32[48,1024]{1,0:T(8,128)} %get-tuple-element.9.in_ref, f32[22,1024]{1,0:T(8,128)} %get-tuple-element.10.out_ref), custom_call_target="tpu_custom_call" | custom-call | tf_op jit(solution)/shard_map/close/pallas_call | solution.py:507

commit v6 on v5

--- a/solution.py
+++ b/solution.py
@@ -247,11 +247,11 @@
         g.foreign()
     ffn(0)
     gi.light_near()
+    gi.heavy_own()
     ffn(1)
     gi.light_far()
     go_.light_near()
     ffn(2)
-    gi.heavy_own()
     go_.light_far()
     ffn(3)
     gi.heavy_other(0)
@@ -301,10 +301,10 @@
     ps[t] = dot_t(pact[1 - c, t], wout[...]).astype(BF16)
     go(ps.at[t], pr.at[t], xs.at[1], xr.at[1], sib)
     got(pr.at[1 - t], xs.at[0], xr.at[0])
-    halves = (slice(0, 64), slice(64, 128))
-    for r, rows in enumerate(halves):
+    pieces = [slice(32 * r, 32 * r + 32) for r in range(4)]
+    for r, rows in enumerate(pieces):
         pzs[rows] = (predo[1 - t, rows] + pr[1 - t, rows].astype(F32)).astype(BF16)
-        go(pzs.at[rows], pzr.at[rows], xs.at[2 + 4 * r], xr.at[2 + 4 * r], zpart)
+        go(pzs.at[rows], pzr.at[rows], xs.at[6 + r], xr.at[6 + r], zpart)
     predo[t] = dot_t(pact[c, t], wout[...])
     for p in range(2):
         for j in range(6):
@@ -329,15 +329,15 @@
     inv_target = lax.rsqrt(jnp.sum(tgt * tgt, axis=1, keepdims=True) + 1e-06)
     got(pr.at[t], xs.at[1], xr.at[1])
     weight = (0.5 + steps[0].astype(F32) / TSTEPS) * ENC
-    for r, rows in enumerate(halves):
-        got(pzr.at[rows], xs.at[2 + 4 * r], xr.at[2 + 4 * r])
+    for r, rows in enumerate(pieces):
+        got(pzr.at[rows], xs.at[6 + r], xr.at[6 + r])
         pred = predo[t, rows] + pr[t, rows].astype(F32) + pzr[rows].astype(F32)
         ry = lax.rsqrt(jnp.sum(pred * pred, axis=1, keepdims=True) + 1e-06)
         rz = inv_target[rows]
         cosine = jnp.sum(pred * tgt[rows], axis=1, keepdims=True) * ry * rz
         dp_all[c, t, rows] = (-weight * (rz * ry * tgt[rows] - cosine * ry * ry * pred)).astype(BF16)
         part = dp_all.at[c, t, rows]
-        go(part, part, xs.at[3 + 4 * r], xr.at[3 + 4 * r], zpart)
+        go(part, part, xs.at[10 + r], xr.at[10 + r], zpart)
     go(dp_all.at[c, t], dp_all.at[c, t], xs.at[4], xr.at[4], sib)
 
     def back(h, p):
@@ -389,18 +389,18 @@
     def _():
         ours()
 
-    for r, rows in enumerate(halves):
+    for r, rows in enumerate(pieces):
         part = dp_all.at[c, 1 - t, rows]
-        got(part, xs.at[3 + 4 * r], xr.at[3 + 4 * r])
-        go(part, part, xs.at[5 + 3 * r], xr.at[5 + 3 * r], sib)
+        got(part, xs.at[10 + r], xr.at[10 + r])
+        go(part, part, xs.at[14 + r], xr.at[14 + r], sib)
 
     @pl.when(early)
     def _():
         send_ours()
 
     back(c, 1 - t)
-    for r, rows in enumerate(halves):
-        got(dp_all.at[1 - c, 1 - t, rows], xs.at[5 + 3 * r], xr.at[5 + 3 * r])
+    for r, rows in enumerate(pieces):
+        got(dp_all.at[1 - c, 1 - t, rows], xs.at[14 + r], xr.at[14 + r])
     back(1 - c, 1 - t)
 
     @pl.when(early)
@@ -540,7 +540,7 @@
         V((3, 80, 512), BF16), V((3, 80, 512), BF16),
         V((4, 256, 768), BF16), V((4, 256, 768), BF16), V((4, 256, 768), BF16),
         D((2, NCH)), D((7,)), D((26,)), D((26,)), D((26,)), D((26,)),
-        D((9,)), D((9,)), D((8,)), D((8,)), D((30,)), D((30,)), D((2,)), D((2,)),
+        D((18,)), D((18,)), D((8,)), D((8,)), D((30,)), D((30,)), D((2,)), D((2,)),
     ]
     zs, zr, in_grad, out_grad = pl.pallas_call(
         kernel,

time: 106 us -> 106 us (level)
  no operation moved by 1% of the time
where the time goes in v6:
time: 106 us
  Pallas kernels  105 us (99%)
  between operations  1.29 us (1%)
    pallas_call x1, Pallas kernels, on_device(): pl.pallas_call(kernel, out_shape=(jax.ShapeDtypeStruct((256, HID), BF16),...  101 us
    pallas_call x1, Pallas kernels, close(): pl.pallas_call(close_kernel, grid=(2,), out_shape=(jax.ShapeDtypeStruct((...  3.36 us

profile of v6, /device:TPU:1, one launch (start us, length us, event | category | flops | bytes accessed | tf_op | source)
XLA Modules:
  0.0 106.0 jit_solution(4161058947660219127)
XLA Ops:
  1.3 101.4 %fused.1 = (bf16[256,3072]{1,0:T(8,128)(2,1)}, bf16[256,3072]{1,0:T(8,128)(2,1)}, f32[48,1024]{1,0:T(8,128)}, f32[22,1024]{1,0:T(8,128)}) custom-call(bf16[256,1408]{1,0:T(8,128)(2,1)} %enc.1, s32[256]{0:T(256)} %order.1, f32[1408]{0:T(1024)} %ng.1, f32[1408]{0:T(1024)} %fg.1, s32[1]{0:T(128)S(6)} %copy.13.steps, bf16[192,1024]{1,0:T(8,128)(2,1)} %wi.1, ...), custom_call_target="tpu_custom_call" | custom-call | tf_op jit(solution)/shard_map/fused/pallas_call | solution.py:545
  102.7 3.4 %close.1 = (f32[256,3072]{1,0:T(8,128)}, f32[48,1024]{1,0:T(8,128)}, f32[22,1024]{1,0:T(8,128)}) custom-call(bf16[256,3072]{1,0:T(8,128)(2,1)} %get-tuple-element.7.a, bf16[256,3072]{1,0:T(8,128)(2,1)} %get-tuple-element.8.b, f32[48,1024]{1,0:T(8,128)} %get-tuple-element.9.in_ref, f32[22,1024]{1,0:T(8,128)} %get-tuple-element.10.out_ref), custom_call_target="tpu_custom_call" | custom-call | tf_op jit(solution)/shard_map/close/pallas_call | solution.py:507
